TPU v7x, 32 devices: a whole 2x2x4 slice. The times are simulated.
32 devices in a mesh: frames: 8 (over y, x, core), pairs: 4 (over z).
Axes of the slice: x: 2, y: 2, z: 4, core: 2. Of those that a mesh axis runs over, the one named last changes fastest.
Arguments:
- coords: float32 [4096, 3, 384], P('frames'), may hold values from -3 to 3
- pair_first: int32 [256], P('pairs'), may hold values from 0 to 383
- pair_second: int32 [32768], P('pairs'), may hold values from 0 to 383
- enc_weight: bfloat16 [64, 32768], P(None, 'pairs'), may hold values from -0.03125 to 0.03125
- enc_bias: float32 [64], replicated, may hold values from -4 to 4
- dec_weight: bfloat16 [64, 32768], P(None, 'pairs'), may hold values from -0.75 to 0.75
- dec_bias: float32 [32768], P('pairs'), may hold values from -3 to 3
- lag_frames: int32 [1], replicated, may hold values from 256 to 512
Outputs:
- grad_enc: float32 [64, 32768], P(None, 'pairs')
- grad_dec: float32 [64, 32768], P(None, 'pairs')
Inputs may be any that keep to these rules, and one draw needn't show every extreme that they name: Residue numbers; pair p joins residue pair_first[p // 128] with residue pair_second[p].
All inputs are finite; a program needn't handle non-finite values.
Results may differ from a plain program's by a relative error of at most 0.0003.
Values may be sent and summed in bfloat16 or wider, within the bound.
A program may use at most 192 MiB of HBM per device.

v0:
```python
from functools import partial

import jax
import jax.numpy as jnp
from jax import lax
from jax.sharding import PartitionSpec as P

cutoff_dist = 2.3
softness = 0.4


def from_behind(block, axis, distance):
    devices = range(lax.axis_size(axis))
    route = [(i - distance, i) for i in devices if i - distance in devices]
    return lax.ppermute(block, axis, route)


def contact_rows(frame_block, first_res, second):
    near = jnp.take(frame_block, first_res, axis=2)
    far = jnp.take(frame_block, second, axis=2)
    far = far.reshape(far.shape[0], 3, first_res.shape[0], 128)
    offset = far - near[..., None]
    distance = jnp.sqrt(jnp.sum(offset * offset, axis=1))
    value = jax.nn.sigmoid((cutoff_dist - distance) / softness)
    return value.reshape(frame_block.shape[0], -1).astype(jnp.bfloat16)


def all_contacts(coords, first_res, second):
    frame_rows = coords.shape[0]
    block_rows = min(128, frame_rows)
    grouped = coords.reshape(frame_rows // block_rows, block_rows, coords.shape[1], coords.shape[2])
    result = lax.map(partial(contact_rows, first_res=first_res, second=second), grouped)
    return result.reshape(frame_rows, -1)


def later_rows(own, following, row_ids, frame_rows):
    own_part = jnp.take(own, jnp.minimum(row_ids, frame_rows - 1), axis=0)
    next_part = jnp.take(following, jnp.maximum(row_ids - frame_rows, 0), axis=0)
    inside = (row_ids < frame_rows).reshape((-1,) + (1,) * (own.ndim - 1))
    return jnp.where(inside, own_part, next_part)


def local(coords, pair_first, pair_second, enc_weight, enc_bias, dec_weight, dec_bias, lag_frames):
    frame_rows = coords.shape[0]
    total_frames = frame_rows * lax.axis_size("frames")
    shift_now = lag_frames[0]
    own_contacts = all_contacts(coords, pair_first, pair_second)
    following = from_behind(own_contacts, "frames", -1)
    partial_sum = lax.dot_general(
        enc_weight, own_contacts, (((1,), (1,)), ((), ())), preferred_element_type=jnp.float32
    )
    share_sum = lax.psum_scatter(partial_sum, "pairs", scatter_dimension=1, tiled=True)
    share_latent = jnp.tanh(share_sum + enc_bias[:, None])
    latent = lax.all_gather(share_latent, "pairs", axis=1, tiled=True)
    latent_bf = latent.astype(jnp.bfloat16)
    scale_factor = 1.0 / jnp.sqrt(jnp.float32(total_frames) - shift_now.astype(jnp.float32))
    block_rows = min(512, frame_rows)
    block_count = frame_rows // block_rows
    first_frame = lax.axis_index("frames") * frame_rows

    def decode_block(grad_sum, block_idx):
        begin_row = block_idx * block_rows
        local_ids = begin_row + jnp.arange(block_rows, dtype=jnp.int32)
        row_ids = local_ids + shift_now
        target = later_rows(own_contacts, following, row_ids, frame_rows)
        decoded = (
            lax.dot_general(
                latent_bf, dec_weight, (((0,), (0,)), ((), ())), preferred_element_type=jnp.float32
            )
            + dec_bias[None, :]
        )
        usable = first_frame + local_ids + shift_now < total_frames
        err_bf = jnp.where(
            usable[:, None], (decoded - target.astype(jnp.float32)) * scale_factor, 0.0
        ).astype(jnp.bfloat16)
        grad_sum = grad_sum + jnp.dot(latent_bf, err_bf, preferred_element_type=jnp.float32)
        back_block = lax.dot_general(
            dec_weight, err_bf, (((1,), (1,)), ((), ())), preferred_element_type=jnp.float32
        )
        return (grad_sum, back_block)

    zeros = jnp.zeros((latent.shape[0], dec_weight.shape[1]), jnp.float32)
    grad_dec, back_blocks = lax.scan(decode_block, zeros, jnp.arange(block_count, dtype=jnp.int32))
    back_terms = jnp.transpose(back_blocks, (1, 0, 2)).reshape(latent.shape[0], frame_rows)
    backward = lax.psum(back_terms, "pairs")
    hidden_bf = (backward * (1.0 - latent * latent)).astype(jnp.bfloat16)
    grad_enc = jnp.dot(hidden_bf, own_contacts, preferred_element_type=jnp.float32)
    grad_dec, grad_enc = lax.psum((grad_dec, grad_enc), "frames")
    return (grad_enc, grad_dec)


def solution(mesh):
    placed = (
        P("frames", None, None),
        P("pairs"),
        P("pairs"),
        P(None, "pairs"),
        P(),
        P(None, "pairs"),
        P("pairs"),
        P(),
    )
    return jax.shard_map(
        local,
        mesh=mesh,
        in_specs=placed,
        out_specs=(P(None, "pairs"), P(None, "pairs")),
        check_vma=False,
    )
```

profile of v0, /device:TPU:0, one launch (start us, length us, event | category | flops | bytes accessed | tf_op | source)
XLA Modules:
  0.0 641.9 jit_solution(4897206884859984272)
XLA Ops:
  7.2 362.0 %while.2 = (s32[]{:T(128)}, bf16[4,128,8192]{2,1,0:T(8,128)(2,1)}, s32[8192]{0:T(1024)}, f32[4,128,3,384]{3,1,0,2:T(8,128)}, s32[64]{0:T(128)}, /*index=5*/s32[]{:T(128)}) while((s32[]{:T(128)}, bf16[4,128,8192]{2,1,0:T(8,128)(2,1)}, s32[8192]{0:T(1024)}, f32[4,128,3,384]{3,1,0,2:T(8,128)}, s32[64]{0:T(128)}, /*index=5*/s32[]{:T(128)}) %tuple.40), condition=%wide.region_2.3_spmd, body=%wide.region_0.2_spmd.sunk | while | flops 17933888 | bytes 85054936 | solution.py:32
  12.5 59.6 %gather_fusion = f32[8192,128,3]{1,2,0:T(4,128)} fusion(f32[128,3,384]{0,1,2:T(4,128)S(1)} %bitcast.54, s32[8192]{0:T(1024)S(1)} %broadcast_clamp_fusion.2), kind=kCustom, calls=%fused_computation.clone.1 | custom fusion | bytes 25198592 | tf_op jit(solution)/shard_map/while/body/eval_jaxpr/jit(_take)/gather | solution.py:20
  72.1 11.1 %copy.28 = f32[128,3,8192]{0,2,1:T(8,128)} copy(f32[128,3,8192]{0,1,2:T(4,128)} %bitcast.55) | data formatting | bytes 25165824 | tf_op jit(solution)/shard_map/while/body/eval_jaxpr/jit(_take)/gather | solution.py:20
  83.2 6.6 %multiply_reduce_fusion.2 = f32[128,64,128]{0,2,1:T(8,128)S(1)} fusion(f32[128,3,64,128]{0,3,2,1:T(8,128)} %bitcast.56, f32[128,3,64]{0,2,1:T(8,128)S(1)} %copy.29, pred[64,128]{1,0:T(8,128)(4,1)S(1)} %and_bitcast_fusion.2), kind=kLoop, calls=%fused_computation.4.clone.1 | loop fusion | flops 11534336 | bytes 16883712 | tf_op jit(solution)/shard_map/while/body/eval_jaxpr/reduce_sum | solution.py:23
  94.7 3.1 constant_dynamic-update-slice_fusion.2
  103.0 59.6 %gather_fusion = f32[8192,128,3]{1,2,0:T(4,128)} fusion(f32[128,3,384]{0,1,2:T(4,128)S(1)} %bitcast.54, s32[8192]{0:T(1024)S(1)} %broadcast_clamp_fusion.2), kind=kCustom, calls=%fused_computation.clone.1 | custom fusion | bytes 25198592 | tf_op jit(solution)/shard_map/while/body/eval_jaxpr/jit(_take)/gather | solution.py:20
  162.6 11.1 %copy.28 = f32[128,3,8192]{0,2,1:T(8,128)} copy(f32[128,3,8192]{0,1,2:T(4,128)} %bitcast.55) | data formatting | bytes 25165824 | tf_op jit(solution)/shard_map/while/body/eval_jaxpr/jit(_take)/gather | solution.py:20
  173.7 6.6 %multiply_reduce_fusion.2 = f32[128,64,128]{0,2,1:T(8,128)S(1)} fusion(f32[128,3,64,128]{0,3,2,1:T(8,128)} %bitcast.56, f32[128,3,64]{0,2,1:T(8,128)S(1)} %copy.29, pred[64,128]{1,0:T(8,128)(4,1)S(1)} %and_bitcast_fusion.2), kind=kLoop, calls=%fused_computation.4.clone.1 | loop fusion | flops 11534336 | bytes 16883712 | tf_op jit(solution)/shard_map/while/body/eval_jaxpr/reduce_sum | solution.py:23
  185.2 3.1 constant_dynamic-update-slice_fusion.2
  193.4 59.6 %gather_fusion = f32[8192,128,3]{1,2,0:T(4,128)} fusion(f32[128,3,384]{0,1,2:T(4,128)S(1)} %bitcast.54, s32[8192]{0:T(1024)S(1)} %broadcast_clamp_fusion.2), kind=kCustom, calls=%fused_computation.clone.1 | custom fusion | bytes 25198592 | tf_op jit(solution)/shard_map/while/body/eval_jaxpr/jit(_take)/gather | solution.py:20
  253.0 11.1 %copy.28 = f32[128,3,8192]{0,2,1:T(8,128)} copy(f32[128,3,8192]{0,1,2:T(4,128)} %bitcast.55) | data formatting | bytes 25165824 | tf_op jit(solution)/shard_map/while/body/eval_jaxpr/jit(_take)/gather | solution.py:20
  264.1 6.6 %multiply_reduce_fusion.2 = f32[128,64,128]{0,2,1:T(8,128)S(1)} fusion(f32[128,3,64,128]{0,3,2,1:T(8,128)} %bitcast.56, f32[128,3,64]{0,2,1:T(8,128)S(1)} %copy.29, pred[64,128]{1,0:T(8,128)(4,1)S(1)} %and_bitcast_fusion.2), kind=kLoop, calls=%fused_computation.4.clone.1 | loop fusion | flops 11534336 | bytes 16883712 | tf_op jit(solution)/shard_map/while/body/eval_jaxpr/reduce_sum | solution.py:23
  275.6 3.1 constant_dynamic-update-slice_fusion.2
  283.9 59.6 %gather_fusion = f32[8192,128,3]{1,2,0:T(4,128)} fusion(f32[128,3,384]{0,1,2:T(4,128)S(1)} %bitcast.54, s32[8192]{0:T(1024)S(1)} %broadcast_clamp_fusion.2), kind=kCustom, calls=%fused_computation.clone.1 | custom fusion | bytes 25198592 | tf_op jit(solution)/shard_map/while/body/eval_jaxpr/jit(_take)/gather | solution.py:20
  343.5 11.1 %copy.28 = f32[128,3,8192]{0,2,1:T(8,128)} copy(f32[128,3,8192]{0,1,2:T(4,128)} %bitcast.55) | data formatting | bytes 25165824 | tf_op jit(solution)/shard_map/while/body/eval_jaxpr/jit(_take)/gather | solution.py:20
  354.6 6.6 %multiply_reduce_fusion.2 = f32[128,64,128]{0,2,1:T(8,128)S(1)} fusion(f32[128,3,64,128]{0,3,2,1:T(8,128)} %bitcast.56, f32[128,3,64]{0,2,1:T(8,128)S(1)} %copy.29, pred[64,128]{1,0:T(8,128)(4,1)S(1)} %and_bitcast_fusion.2), kind=kLoop, calls=%fused_computation.4.clone.1 | loop fusion | flops 11534336 | bytes 16883712 | tf_op jit(solution)/shard_map/while/body/eval_jaxpr/reduce_sum | solution.py:23
  366.1 3.1 constant_dynamic-update-slice_fusion.2
  370.5 6.9 %convolution_bitcast_fusion.1 = f32[64,512]{1,0:T(8,128)} fusion(bf16[512,8192]{1,0:T(8,128)(2,1)} %bitcast.58, bf16[64,8192]{1,0:T(8,128)(2,1)} %param.15), kind=kOutput, calls=%fused_computation.21 | convolution fusion | flops 536870912 | bytes 9568256 | tf_op jit(solution)/shard_map/dot_general | solution.py:49
  378.4 19.9 %gather_fusion.2 = bf16[512,8192]{1,0:T(8,128)(2,1)} fusion(bf16[512,8192]{1,0:T(8,128)(2,1)} %bitcast.59, s32[1024]{0:T(1024)S(1)} %pad_clamp_fusion.2), kind=kCustom, calls=%fused_computation.2.clone | custom fusion | bytes 16779264 | tf_op jit(solution)/shard_map/while/body/eval_jaxpr/jit(_take)/gather | solution.py:37
  398.3 5.2 reduce-scatter.2.cloned.1.call-done
  404.3 13.7 %all_gather.3 = f32[64,512]{1,0:T(8,128)S(1)} all-gather(f32[64,128]{1,0:T(8,128)S(1)} %add_tanh_fusion), channel_id=1, replica_groups=mesh['frames'=8,'pairs'=4] {'pairs'}, dimensions={1}, use_global_device_ids=true | all-gather | bytes 163840 | tf_op jit(solution)/shard_map/all_gather | solution.py:54
  418.0 8.1 %fusion.5 = f32[512,8192]{1,0:T(8,128)} fusion(bf16[64,8192]{1,0:T(8,128)(2,1)S(1)} %copy-done, f32[64,512]{1,0:T(8,128)S(1)} %all_gather.3), kind=kOutput, calls=%fused_computation.27 | convolution fusion | flops 536903680 | bytes 17956864 | tf_op jit(solution)/shard_map/while/body/eval_jaxpr/dot_general | solution.py:67
  426.1 20.2 %gather_fusion.3 = bf16[512,8192]{1,0:T(8,128)(2,1)} fusion(bf16[512,8192]{1,0:T(8,128)(2,1)} %collective-permute-done, s32[1024]{0:T(1024)S(1)} %pad_clamp_fusion.1), kind=kCustom, calls=%fused_computation.3.clone | custom fusion | bytes 16779264 | tf_op jit(solution)/shard_map/while/body/eval_jaxpr/jit(_take)/gather | solution.py:38
  446.3 14.2 %select_convert_fusion = bf16[512,8192]{1,0:T(8,128)(2,1)S(1)} fusion(f32[512,8192]{1,0:T(8,128)} %fusion.5, bf16[512,8192]{1,0:T(8,128)(2,1)} %gather_fusion.3, bf16[512,8192]{1,0:T(8,128)(2,1)} %gather_fusion.2, f32[]{:T(128)S(6)} %sqrt.15, f32[8192]{0:T(1024)S(1)} %copy-done.2, pred[512]{0:T(512)(128)(4,1)S(1)} %get-tuple-element.89, ...), kind=kLoop, calls=%fused_computation.18 | loop fusion | flops 37748736 | bytes 41977860 | tf_op jit(solution)/shard_map/while/body/eval_jaxpr/convert_element_type | solution.py:75
  460.5 3.2 copy-done.1
  463.7 3.3 convolution_bitcast_fusion
  467.4 6.3 fusion.3
  473.6 68.3 %all-reduce.4.cloned.1.call-done = f32[64,512]{1,0:T(8,128)} async-done(((f32[64,512]{1,0:T(8,128)}), f32[64,512]{1,0:T(8,128)}) %all-reduce.4.cloned.1.call-update) | async-done | bytes 131088 | tf_op jit(solution)/shard_map/psum | solution.py:85
  541.9 6.3 fusion.1
  548.3 81.0 %all-reduce.6.cloned.1.call-done = (f32[64,8192]{1,0:T(8,128)}, f32[64,8192]{1,0:T(8,128)}) async-done(((f32[64,8192]{1,0:T(8,128)}, f32[64,8192]{1,0:T(8,128)}), (f32[64,8192]{1,0:T(8,128)}, f32[64,8192]{1,0:T(8,128)})) %all-reduce.6.cloned.1.call-update) | async-done | bytes 4194320 | tf_op jit(solution)/shard_map/psum | solution.py:88
  629.3 3.1 copy.44
  632.4 3.1 copy.45
  (75 shorter events, 42.9 us)
Async XLA Ops:
  7.2 410.9 %copy-start = (bf16[64,8192]{1,0:T(8,128)(2,1)S(1)}, bf16[64,8192]{1,0:T(8,128)(2,1)}, u32[]{:S(2)}) copy-start(bf16[64,8192]{1,0:T(8,128)(2,1)} %param.17) | copy-start | bytes 3145732
  7.2 396.3 %reduce-scatter.2.cloned.1.call-start = ((), (), s32[]{:S(2)}) async-start(), calls=%async_computation.1 | async-start | bytes 163840 | tf_op jit(solution)/shard_map/reduce_scatter | solution.py:52
  369.2 56.9 %collective-permute-start = (bf16[512,8192]{1,0:T(8,128)(2,1)}, bf16[512,8192]{1,0:T(8,128)(2,1)}, u32[]{:S(2)}, u32[]{:S(2)}) collective-permute-start(bf16[512,8192]{1,0:T(8,128)(2,1)} %bitcast.57), channel_id=1, source_target_pairs={{4,0},{8,4},{12,8},{16,12},{20,16},{24,20},{28,24},{5,1},{9,5},{13... | collective-permute-start | bytes 25165832 | tf_op jit(solution)/shard_map/ppermute | solution.py:15
  377.4 164.5 %all-reduce.4.cloned.1.call-start = ((), (), s32[]{:S(2)}) async-start(), calls=%async_computation.2 | async-start | bytes 262144 | tf_op jit(solution)/shard_map/psum | solution.py:85
  378.4 25.1 %copy-start.3 = (f32[64]{0:T(128)S(1)}, f32[64]{0:T(128)}, u32[]{:S(2)}) copy-start(f32[64]{0:T(128)} %param.16) | copy-start | bytes 772
  426.1 20.2 %copy-start.2 = (f32[8192]{0:T(1024)S(1)}, f32[8192]{0:T(1024)}, u32[]{:S(2)}) copy-start(f32[8192]{0:T(1024)} %param.18) | copy-start | bytes 98308
  460.5 3.2 copy-start.1
  467.1 162.2 %all-reduce.6.cloned.1.call-start = ((), (), s32[]{:S(2)}) async-start(), calls=%async_computation.3 | async-start | bytes 8388608 | tf_op jit(solution)/shard_map/psum | solution.py:88
Sparse Core Ops, SparseCore 0:
  377.6 25.8 reduce-scatter.1
  467.2 74.6 all-reduce.3
  548.4 80.8 all-reduce.5
where the time goes:
time: 644 us; the launch traced here: 642 us
  local copies, waits for them, and re-layouts  364 us (57%)
  waiting for transfers between devices  154 us (24%)
  other arithmetic  61.7 us (10%)
  matrix products  31 us (5%)
  between operations  14.5 us (2%)
  blocking collectives  13.7 us (2%)
    gather x8, local copies, waits for them, and re-layouts, contact_rows(): far = jnp.take(frame_block, second, axis=2)  283 us
    psum x1, waiting for transfers between devices, local(): grad_dec, grad_enc = lax.psum((grad_dec, grad_enc), 'frames')  81 us
    psum x1, waiting for transfers between devices, local(): backward = lax.psum(back_terms, 'pairs')  68.3 us
    reduce_sum x4, other arithmetic, contact_rows(): distance = jnp.sqrt(jnp.sum(offset * offset, axis=1))  26.4 us
    dynamic_update_slice x8, local copies, waits for them, and re-layouts, all_contacts(): lax.map(partial(contact_rows, first_res=first_res, second=second), grouped)  24 us
    gather x1, local copies, waits for them, and re-layouts, later_rows(): jnp.take(following, jnp.maximum(row_ids - frame_rows, 0), axis=0)  20.2 us
    gather x1, local copies, waits for them, and re-layouts, later_rows(): own_part = jnp.take(own, jnp.minimum(row_ids, frame_rows - 1), axis=0)  19.9 us
    convert_element_type x1, other arithmetic, decode_block(): err_bf = jnp.where(usable[:, None], (decoded - target.astype(jnp.float32)...  14.2 us
  transfers between devices with their start and end apart: 4, of which 3 were waited for; matrix products, arithmetic and copies ran while one was open for 7% of the time, Pallas kernels for 0%

commit v1 on v0

v1 whole, which is shorter than its diff:
```python
from functools import partial

import jax
import jax.numpy as jnp
from jax import lax
from jax.experimental import pallas as pl
from jax.experimental.pallas import tpu as pltpu
from jax.sharding import PartitionSpec as P

cutoff_dist = 2.3
softness = 0.4
log2_e = 1.4426950408889634
pieces = 2
unit = 256


def split(value, count):
    parts = []
    rest = value
    for _ in range(count):
        part = rest.astype(jnp.bfloat16)
        parts.append(part)
        rest = rest - part.astype(jnp.float32)
    return parts


def contact_kernel(
    coords_ref, first_ref, second_ref, enc_ref, dec_ref, bias_ref,
    contact_ref, sums_ref, gram_ref, lean_ref, table, weights,
):
    step = pl.program_id(0)
    rows, residues = coords_ref.shape[1], coords_ref.shape[2]

    @pl.when(step == 0)
    def prepare():
        for axis in range(3):
            for i, part in enumerate(split(coords_ref[axis], pieces)):
                table[axis * rows:(axis + 1) * rows, i * residues:(i + 1) * residues] = part
        sums_ref[...] = jnp.zeros_like(sums_ref)
        gram_ref[...] = jnp.zeros_like(gram_ref)
        lean_ref[...] = jnp.zeros_like(lean_ref)

    width = first_ref.shape[1]
    latents = enc_ref.shape[0]
    weights[:latents, :] = enc_ref[...]
    weights[latents:, :] = dec_ref[...]
    gram_ref[...] += lax.dot_general(
        dec_ref[...], dec_ref[...], (((1,), (1,)), ((), ())), preferred_element_type=jnp.float32
    )
    lean = dec_ref[...].astype(jnp.float32) * bias_ref[...]
    for i in range(width // 128):
        lean_ref[...] += lean[:, i * 128:(i + 1) * 128]
    total = jnp.zeros(sums_ref.shape, jnp.float32)
    for i in range(width // unit):
        here = slice(i * unit, (i + 1) * unit)
        ids = lax.broadcasted_iota(jnp.int32, (residues, unit), 0)
        choice = (
            jnp.where(ids == second_ref[:, here], 1.0, 0.0) - jnp.where(ids == first_ref[:, here], 1.0, 0.0)
        ).astype(jnp.bfloat16)
        choice = jnp.concatenate([choice] * pieces, axis=0)
        square = jnp.zeros((rows, unit), jnp.float32)
        for axis in range(3):
            offset = jnp.dot(
                table[axis * rows:(axis + 1) * rows, :], choice, preferred_element_type=jnp.float32
            )
            square = square + offset * offset
        distance = square * lax.rsqrt(jnp.maximum(square, 1e-30))
        power = jnp.exp2(distance * (log2_e / softness) - cutoff_dist * log2_e / softness)
        contact = (1.0 / (1.0 + power)).astype(jnp.bfloat16)
        contact_ref[:, here] = contact
        total = total + lax.dot_general(
            contact, weights[:, here], (((1,), (1,)), ((), ())), preferred_element_type=jnp.float32
        )
    sums_ref[...] += total


def contacts(coords, first, second, enc_weight, dec_weight, dec_bias):
    rows, _, residues = coords.shape
    latents, pairs = enc_weight.shape
    width = min(512, pairs)
    row = pl.BlockSpec((1, width), lambda i: (0, i))
    block = pl.BlockSpec((latents, width), lambda i: (0, i))
    return pl.pallas_call(
        contact_kernel,
        grid=(pairs // width,),
        in_specs=[pl.BlockSpec((3, rows, residues), lambda i: (0, 0, 0)), row, row, block, block, row],
        out_specs=[
            pl.BlockSpec((rows, width), lambda i: (0, i)),
            pl.BlockSpec((rows, 2 * latents), lambda i: (0, 0)),
            pl.BlockSpec((latents, latents), lambda i: (0, 0)),
            pl.BlockSpec((latents, 128), lambda i: (0, 0)),
        ],
        out_shape=[
            jax.ShapeDtypeStruct((rows, pairs), jnp.bfloat16),
            jax.ShapeDtypeStruct((rows, 2 * latents), jnp.float32),
            jax.ShapeDtypeStruct((latents, latents), jnp.float32),
            jax.ShapeDtypeStruct((latents, 128), jnp.float32),
        ],
        scratch_shapes=[
            pltpu.VMEM((3 * rows, pieces * residues), jnp.bfloat16),
            pltpu.VMEM((2 * latents, width), jnp.bfloat16),
        ],
        compiler_params=pltpu.CompilerParams(vmem_limit_bytes=50 * 2**20),
        name="contacts",
    )(jnp.transpose(coords, (1, 0, 2)), first, second, enc_weight, dec_weight, dec_bias)


def grad_kernel(left_ref, mix_ref, scale_ref, contact_ref, dec_ref, bias_ref, enc_out, dec_out):
    latents = dec_ref.shape[0]
    product = jnp.dot(left_ref[...], contact_ref[...], preferred_element_type=jnp.float32)
    dec = dec_ref[...]
    own = jnp.dot(
        jnp.concatenate(split(mix_ref[...], 3), axis=1),
        jnp.concatenate([dec, dec, dec], axis=0),
        preferred_element_type=jnp.float32,
    )
    enc_out[...] = product[:latents]
    dec_out[...] = scale_ref[:, :1] * (own + scale_ref[:, 1:2] * bias_ref[...] - product[latents:])


def grads(left, mix, scale, contact, dec_weight, dec_bias):
    rows, pairs = contact.shape
    latents = dec_weight.shape[0]
    width = min(1024, pairs)
    whole = lambda a: pl.BlockSpec(a.shape, lambda i: (0, 0))
    out = pl.BlockSpec((latents, width), lambda i: (0, i))
    return pl.pallas_call(
        grad_kernel,
        grid=(pairs // width,),
        in_specs=[
            whole(left), whole(mix), whole(scale),
            pl.BlockSpec((rows, width), lambda i: (0, i)), out, pl.BlockSpec((1, width), lambda i: (0, i)),
        ],
        out_specs=[out, out],
        out_shape=[jax.ShapeDtypeStruct((latents, pairs), jnp.float32)] * 2,
        compiler_params=pltpu.CompilerParams(vmem_limit_bytes=40 * 2**20),
        name="grads",
    )(left, mix, scale, contact, dec_weight, dec_bias)


def middle(sums, gram, lean, own_rows, enc_bias, lag):
    rows, latents = sums.shape[0], gram.shape[0]
    devices = lax.axis_size("frames")
    total_frames = rows * devices
    latent = jnp.tanh(sums[:, :latents] + enc_bias[None, :])
    rounded = lax.reduce_precision(latent, 8, 7)
    latent_bf = rounded.astype(jnp.bfloat16)
    seen = sums[:, latents:]
    seen_next = lax.ppermute(seen, "frames", [(i, i - 1) for i in range(1, devices)])
    latent_prev = lax.ppermute(latent_bf, "frames", [(i, i + 1) for i in range(devices - 1)])
    seen_later = lax.dynamic_slice_in_dim(jnp.concatenate([seen, seen_next]), lag, rows, 0)
    latent_earlier = lax.dynamic_slice_in_dim(
        jnp.concatenate([latent_prev, latent_bf]), rows - lag, rows, 0
    )
    usable = (own_rows + lag < total_frames)[:, None]
    scale = 1.0 / jnp.sqrt(jnp.float32(total_frames) - lag.astype(jnp.float32))
    decoded = jnp.dot(rounded, gram, precision=lax.Precision.HIGHEST) + lean[None, :]
    backward = jnp.where(usable, (decoded - seen_later) * scale, 0.0)
    hidden_bf = (backward * (1.0 - latent * latent)).astype(jnp.bfloat16)
    used = jnp.where(usable, latent_bf, jnp.bfloat16(0))
    mix = lax.dot_general(used, used, (((0,), (0,)), ((), ())), preferred_element_type=jnp.float32)
    tilt = jnp.sum(used.astype(jnp.float32), axis=0)
    left = jnp.concatenate([hidden_bf, latent_earlier], axis=1).T
    scales = jnp.concatenate(
        [jnp.full((latents, 1), scale), tilt[:, None], jnp.zeros((latents, 126), jnp.float32)], axis=1
    )
    return left, mix, scales


def local(coords, pair_first, pair_second, enc_weight, enc_bias, dec_weight, dec_bias, lag_frames):
    rows = coords.shape[0]
    latents, pairs = enc_weight.shape
    first = jnp.broadcast_to(pair_first[:, None], (pairs // 128, 128)).reshape(1, pairs)
    bias = dec_bias.reshape(1, pairs)
    contact, sums, gram, lean = contacts(
        coords, first, pair_second.reshape(1, pairs), enc_weight, dec_weight, bias
    )
    small = jnp.concatenate([sums.reshape(-1), gram.reshape(-1), jnp.sum(lean, axis=1)])
    small = lax.psum(small, "pairs")
    sums = small[: sums.size].reshape(sums.shape)
    gram = small[sums.size : sums.size + gram.size].reshape(gram.shape)
    lean = small[sums.size + gram.size :]
    own_rows = lax.axis_index("frames") * rows + jnp.arange(rows, dtype=jnp.int32)
    left, mix, scales = middle(sums, gram, lean, own_rows, enc_bias, lag_frames[0])
    both = grads(left, mix, scales, contact, dec_weight, bias)
    return tuple(lax.psum(tuple(both), "frames"))


def solution(mesh):
    placed = (
        P("frames", None, None),
        P("pairs"),
        P("pairs"),
        P(None, "pairs"),
        P(),
        P(None, "pairs"),
        P("pairs"),
        P(),
    )
    return jax.shard_map(
        local,
        mesh=mesh,
        in_specs=placed,
        out_specs=(P(None, "pairs"), P(None, "pairs")),
        check_vma=False,
    )
```

time: 644 us -> 195 us (0.30)
  local copies, waits for them, and re-layouts: 364 us -> 14.3 us
  other arithmetic: 61.7 us -> 1.26 us
  Pallas kernels: 0 us -> 35.7 us
  matrix products: 31 us -> 0.52 us
  waiting for transfers between devices: 154 us -> 125 us
  blocking collectives: 13.7 us -> 0 us
    gather x14 -> x0, local copies, waits for them, and re-layouts: 325 us -> none  [the longest x8 283 us: contact_rows(): far = jnp.take(frame_block, second, axis=2)]
    pallas_call x0 -> x2, Pallas kernels: none -> 35.7 us  [the longest x1 30.6 us: contacts(): pl.pallas_call(contact_kernel, grid=(pairs // width,), in_specs=[pl.Block...]
    dot_general x5 -> x2, matrix products: 31 us -> 0.52 us  [the longest x1 0.37 us: middle(): jnp.dot(rounded, gram, precision=lax.Precision.HIGHEST) + lean[None, :]]
    psum x2, waiting for transfers between devices: 149 us -> 122 us  [the longest x1 84.4 us: local(): return tuple(lax.psum(tuple(both), 'frames'))]
    reduce_sum x4 -> x2, other arithmetic: 26.4 us -> 0.3 us  [the longest x1 0.19 us: middle(): tilt = jnp.sum(used.astype(jnp.float32), axis=0)]
    dynamic_update_slice x8 -> x0, local copies, waits for them, and re-layouts: 24 us -> none  [all_contacts(): lax.map(partial(contact_rows, first_res=first_res, second=second), grouped)]
    convert_element_type x5 -> x0, other arithmetic: 22.2 us -> none  [the longest x1 14.2 us: decode_block(): err_bf = jnp.where(usable[:, None], (decoded - target.astype(jnp.float32)...]
    all_gather x1 -> x0, blocking collectives: 13.7 us -> none  [local(): latent = lax.all_gather(share_latent, 'pairs', axis=1, tiled=True)]
  transfers between devices with their start and end apart: 4 -> 4, of which waited for: 3 -> 3; matrix products, arithmetic and copies ran while one was open for 7% -> 0% of each run, Pallas kernels for 0% -> 0%
where the time goes in v1:
time: 195 us
  waiting for transfers between devices  125 us (64%)
  Pallas kernels  35.7 us (18%)
  between operations  14.9 us (8%)
  local copies, waits for them, and re-layouts  14.3 us (7%)
  starting transfers between devices  2.65 us (1%)
    psum x1, waiting for transfers between devices, local(): return tuple(lax.psum(tuple(both), 'frames'))  84.4 us
    psum x1, waiting for transfers between devices, local(): small = lax.psum(small, 'pairs')  37.6 us
    pallas_call x1, Pallas kernels, contacts(): pl.pallas_call(contact_kernel, grid=(pairs // width,), in_specs=[pl.Block...  30.6 us
    unnamed x22, local copies, waits for them, and re-layouts  12.1 us
    pallas_call x1, Pallas kernels, grads(): pl.pallas_call(grad_kernel, grid=(pairs // width,), in_specs=[whole(left)...  5.13 us
  transfers between devices with their start and end apart: 4, of which 3 were waited for; matrix products, arithmetic and copies ran while one was open for 0% of the time, Pallas kernels for 0%

profile of v1, /device:TPU:0, one launch (start us, length us, event | category | flops | bytes accessed | tf_op | source)
XLA Modules:
  0.0 194.8 jit_solution(11678549335005781976)
XLA Ops:
  7.2 0.0 all-reduce.4.cloned.1.call-start
  7.2 0.7 broadcast_in_dim.41
  7.9 1.2 copy-done.1
  9.2 1.2 copy-done.3
  10.4 0.8 copy-done.4
  11.2 0.8 copy-done.6
  11.9 30.6 %contacts.1 = (bf16[512,8192]{1,0:T(8,128)(2,1)}, f32[512,128]{1,0:T(8,128)S(1)}, f32[64,64]{1,0:T(8,128)S(1)}, f32[64,128]{1,0:T(8,128)S(1)}) custom-call(f32[3,512,384]{2,1,0:T(8,128)} %bitcast.25, s32[1,8192]{1,0:T(1,128)S(1)} %bitcast.23, s32[1,8192]{1,0:T(1,128)S(1)} %bitcast.24, bf16[64,8192]{1,0:T(8,128)(2,1)S(1)} %copy-done.3, ...), custom_call_target="tpu_custom_call" | custom-call | tf_op jit(solution)/shard_map/contacts/pallas_call | solution.py:83
  42.5 0.1 reshape.46
  42.6 0.1 reduce_sum.18
  42.7 0.7 pad_maximum_fusion
  43.5 0.0 all-reduce.6.cloned.1.call-start
  44.3 0.1 pad.2.clone
  44.4 37.6 %all-reduce.4.cloned.1.call-done = f32[69696]{0:T(1024)} async-done(((f32[69696]{0:T(1024)}), f32[69696]{0:T(1024)}) %all-reduce.4.cloned.1.call-update) | async-done | bytes 278800 | tf_op jit(solution)/shard_map/psum | solution.py:179
  82.0 1.0 slice_bitcast_fusion
  82.9 0.1 fusion.14
  83.1 0.1 copy.14
  83.2 0.2 convert_reduce_fusion
  83.4 0.2 fusion.11.mix_ref
  83.6 1.3 collective-permute-start.1
  84.9 0.1 copy.15
  85.0 0.1 copy.13
  85.1 1.3 collective-permute-start
  86.4 0.1 maximum_maximum_fusion.scale_ref
  86.5 0.1 reshape.48
  86.5 0.1 fusion.9
  86.7 3.4 %collective-permute-done = f32[512,64]{0,1:T(8,128)S(1)} collective-permute-done((f32[512,64]{0,1:T(8,128)S(1)}, f32[512,64]{0,1:T(8,128)S(1)}, u32[]{:S(2)}, u32[]{:S(2)}) %collective-permute-start) | collective-permute-done | bytes 131104 | tf_op jit(solution)/shard_map/ppermute | solution.py:149
  90.0 0.4 fusion.5
  90.4 3.4 %copy-done = bf16[512,8192]{1,0:T(8,128)(2,1)S(1)} copy-done((bf16[512,8192]{1,0:T(8,128)(2,1)S(1)}, bf16[512,8192]{1,0:T(8,128)(2,1)}, u32[]{:S(2)}) %copy-start) | copy-done | bytes 8388632
  93.8 5.1 %grads.1 = (f32[64,8192]{1,0:T(8,128)}, f32[64,8192]{1,0:T(8,128)}) custom-call(bf16[128,512]{1,0:T(8,128)(2,1)S(1)} %maximum_bitcast_fusion.left_ref, f32[64,64]{1,0:T(8,128)S(1)} %fusion.11.mix_ref, f32[64,128]{1,0:T(8,128)S(1)} %maximum_maximum_fusion.scale_ref, bf16[512,8192]{1,0:T(8,128)(2,1)S(1)} %copy-done, bf16[64,8192]{1,0:T(8,128)(2,1)S(1)} %copy-done.2, ...), custom_call_target="tpu_custom_call" | custom-call | tf_op jit(solution)/shard_map/grads/pallas_call | solution.py:127
  99.0 84.4 %all-reduce.6.cloned.1.call-done = (f32[64,8192]{1,0:T(8,128)}, f32[64,8192]{1,0:T(8,128)}) async-done(((f32[64,8192]{1,0:T(8,128)}, f32[64,8192]{1,0:T(8,128)}), (f32[64,8192]{1,0:T(8,128)}, f32[64,8192]{1,0:T(8,128)})) %all-reduce.6.cloned.1.call-update) | async-done | bytes 4194320 | tf_op jit(solution)/shard_map/psum | solution.py:186
  183.4 3.2 %copy.20 = f32[64,8192]{1,0:T(8,128)} copy(f32[64,8192]{1,0:T(8,128)} %get-tuple-element.20) | data formatting | bytes 4194304
  186.6 1.3 copy.21
  (24 shorter events, 0.1 us)
Async XLA Ops:
  7.2 74.8 %all-reduce.4.cloned.1.call-start = ((), (), s32[]{:S(2)}) async-start(), calls=%async_computation | async-start | bytes 565248 | tf_op jit(solution)/shard_map/psum | solution.py:179
  7.9 1.2 copy-start.1
  9.2 1.2 copy-start.3
  10.4 0.8 copy-start.4
  11.2 0.8 copy-start.6
  42.5 40.7 %copy-start.8 = (f32[64]{0:T(128)S(1)}, f32[64]{0:T(128)}, u32[]{:S(2)}) copy-start(f32[64]{0:T(128)} %param.12) | copy-start | bytes 772
  43.4 47.0 %copy-start.2 = (bf16[64,8192]{1,0:T(8,128)(2,1)S(1)}, bf16[64,8192]{1,0:T(8,128)(2,1)}, u32[]{:S(2)}) copy-start(bf16[64,8192]{1,0:T(8,128)(2,1)} %dec_ref.3) | copy-start | bytes 3145732
  43.4 47.0 %copy-start.5 = (f32[8192]{0:T(1024)S(1)}, f32[8192]{0:T(1024)}, u32[]{:S(2)}) copy-start(f32[8192]{0:T(1024)} %param.14) | copy-start | bytes 98308
  43.5 139.9 %all-reduce.6.cloned.1.call-start = ((), (), s32[]{:S(2)}) async-start(), calls=%async_computation.1 | async-start | bytes 8388608 | tf_op jit(solution)/shard_map/psum | solution.py:186
  82.0 4.5 %slice-start = ((f32[69696]{0:T(1024)}), f32[4096]{0:T(1024)S(1)}, s32[]{:S(2)}) async-start(f32[69696]{0:T(1024)} %all-reduce.4.cloned.1.call-done), calls=%async_computation.2 | async-start | bytes 32768 | tf_op jit(solution)/shard_map/slice | solution.py:181
  82.0 8.1 %slice-start.1 = ((f32[69696]{0:T(1024)}), f32[64]{0:T(128)S(1)}, s32[]{:S(2)}) async-start(f32[69696]{0:T(1024)} %all-reduce.4.cloned.1.call-done), calls=%async_computation.3 | async-start | bytes 1024 | tf_op jit(solution)/shard_map/slice | solution.py:182
  83.6 3.0 %collective-permute-start.1 = (bf16[512,64]{0,1:T(8,128)(2,1)S(1)}, bf16[512,64]{0,1:T(8,128)(2,1)S(1)}, u32[]{:S(2)}, u32[]{:S(2)}) collective-permute-start(bf16[512,64]{0,1:T(8,128)(2,1)S(1)} %get-tuple-element.17), channel_id=1, source_target_pairs={{0,4},{4,8},{8,12},{12,16},{16,20},{20,24},{24,28},{1,5},{5,9},{9,... | collective-permute-start | bytes 196616 | tf_op jit(solution)/shard_map/ppermute | solution.py:150
  85.1 4.9 %collective-permute-start = (f32[512,64]{0,1:T(8,128)S(1)}, f32[512,64]{0,1:T(8,128)S(1)}, u32[]{:S(2)}, u32[]{:S(2)}) collective-permute-start(f32[512,64]{0,1:T(8,128)S(1)} %copy.15), channel_id=1, source_target_pairs={{4,0},{8,4},{12,8},{16,12},{20,16},{24,20},{28,24},{5,1},{9,5},{13... | collective-permute-start | bytes 393224 | tf_op jit(solution)/shard_map/ppermute | solution.py:149
  90.4 3.4 %copy-start = (bf16[512,8192]{1,0:T(8,128)(2,1)S(1)}, bf16[512,8192]{1,0:T(8,128)(2,1)}, u32[]{:S(2)}) copy-start(bf16[512,8192]{1,0:T(8,128)(2,1)} %get-tuple-element.11.contact_ref) | copy-start | bytes 25165828
  183.4 3.2 %copy-start.7 = (f32[64,8192]{1,0:T(8,128)S(1)}, f32[64,8192]{1,0:T(8,128)}, u32[]{:S(2)}) copy-start(f32[64,8192]{1,0:T(8,128)} %get-tuple-element.21) | copy-start | bytes 6291460
Sparse Core Ops, SparseCore 0:
  43.6 38.3 all-reduce.3
  99.1 84.2 all-reduce.5

commit v2 on v1

v2 whole, which is shorter than its diff:
```python
from functools import partial

import jax
import jax.numpy as jnp
from jax import lax
from jax.experimental import pallas as pl
from jax.experimental.pallas import tpu as pltpu
from jax.sharding import PartitionSpec as P

cutoff_dist = 2.3
softness = 0.4
log2_e = 1.4426950408889634
pieces = 2
unit = 256


def split(value, count):
    parts = []
    rest = value
    for _ in range(count):
        part = rest.astype(jnp.bfloat16)
        parts.append(part)
        rest = rest - part.astype(jnp.float32)
    return parts


def contact_kernel(
    coords_ref, first_ref, second_ref, enc_ref, dec_ref, contact_ref, sums_ref, table, weights
):
    step = pl.program_id(0)
    rows, residues = coords_ref.shape[1], coords_ref.shape[2]

    @pl.when(step == 0)
    def prepare():
        for axis in range(3):
            for i, part in enumerate(split(coords_ref[axis], pieces)):
                table[axis * rows:(axis + 1) * rows, i * residues:(i + 1) * residues] = part
        sums_ref[...] = jnp.zeros_like(sums_ref)

    width = first_ref.shape[1]
    latents = enc_ref.shape[0]
    weights[:latents, :] = enc_ref[...]
    weights[latents:, :] = dec_ref[...]
    total = jnp.zeros(sums_ref.shape, jnp.float32)
    for i in range(width // unit):
        here = slice(i * unit, (i + 1) * unit)
        ids = lax.broadcasted_iota(jnp.int32, (residues, unit), 0)
        choice = (
            jnp.where(ids == second_ref[:, here], 1.0, 0.0) - jnp.where(ids == first_ref[:, here], 1.0, 0.0)
        ).astype(jnp.bfloat16)
        choice = jnp.concatenate([choice] * pieces, axis=0)
        square = jnp.zeros((rows, unit), jnp.float32)
        for axis in range(3):
            offset = jnp.dot(
                table[axis * rows:(axis + 1) * rows, :], choice, preferred_element_type=jnp.float32
            )
            square = square + offset * offset
        distance = square * lax.rsqrt(jnp.maximum(square, 1e-30))
        power = jnp.exp2(distance * (log2_e / softness) - cutoff_dist * log2_e / softness)
        contact = (1.0 / (1.0 + power)).astype(jnp.bfloat16)
        contact_ref[:, here] = contact
        total = total + lax.dot_general(
            contact, weights[:, here], (((1,), (1,)), ((), ())), preferred_element_type=jnp.float32
        )
    sums_ref[...] += total


def contacts(coords, first, second, enc_weight, dec_weight):
    rows, _, residues = coords.shape
    latents, pairs = enc_weight.shape
    width = min(512, pairs)
    row = pl.BlockSpec((1, width), lambda i: (0, i))
    block = pl.BlockSpec((latents, width), lambda i: (0, i))
    return pl.pallas_call(
        contact_kernel,
        grid=(pairs // width,),
        in_specs=[pl.BlockSpec((3, rows, residues), lambda i: (0, 0, 0)), row, row, block, block],
        out_specs=[
            pl.BlockSpec((rows, width), lambda i: (0, i)),
            pl.BlockSpec((rows, 2 * latents), lambda i: (0, 0)),
        ],
        out_shape=[
            jax.ShapeDtypeStruct((rows, pairs), jnp.bfloat16),
            jax.ShapeDtypeStruct((rows, 2 * latents), jnp.float32),
        ],
        scratch_shapes=[
            pltpu.VMEM((3 * rows, pieces * residues), jnp.bfloat16),
            pltpu.VMEM((2 * latents, width), jnp.bfloat16),
        ],
        compiler_params=pltpu.CompilerParams(vmem_limit_bytes=50 * 2**20),
        cost_estimate=pl.CostEstimate(
            flops=2 * 3 * rows * pieces * residues * pairs,
            bytes_accessed=4 * rows * pairs,
            transcendentals=3 * rows * pairs,
        ),
        name="contacts",
    )(jnp.transpose(coords, (1, 0, 2)), first, second, enc_weight, dec_weight)


def tail_kernel(
    chunks, lag_ref, scale_ref, enc_bias_ref, sums_ref, gram_ref, lean_ref, dec_ref, bias_ref, contact_any,
    out_ref, contact_ref, zrecv, whole, seen_send, seen_recv, lat_send, lat_recv, left_ref, partial_sum, arrived,
    contact_sem, z_send, z_recv, side_send, side_recv, half_send, half_recv, full_send, full_recv,
):
    frames, pairs = lax.axis_size("frames"), lax.axis_size("pairs")
    me, depth = lax.axis_index("frames"), lax.axis_index("pairs")
    bits = frames.bit_length() - 1
    rows, latents = sums_ref.shape[0], dec_ref.shape[0]
    part = rows // pairs
    width = dec_ref.shape[1] // chunks
    shard = width // frames
    half = rows // 2

    def partner(bit):
        return me + (1 << bit) - 2 * (1 << bit) * (lax.div(me, 1 << bit) % 2)

    def bit_of(bit):
        return lax.div(me, 1 << bit) % 2

    following, previous = lax.rem(me + 1, frames), lax.rem(me + frames - 1, frames)

    load = pltpu.make_async_copy(contact_any, contact_ref, contact_sem)
    load.start()
    barrier = pltpu.get_barrier_semaphore()
    for step in range(1, pairs):
        pl.semaphore_signal(
            barrier, inc=1, device_id={"pairs": lax.rem(depth + step, pairs)}, device_id_type=pl.DeviceIdType.MESH
        )
    for other in [following, previous] + [partner(b) for b in range(bits)]:
        pl.semaphore_signal(barrier, inc=1, device_id={"frames": other}, device_id_type=pl.DeviceIdType.MESH)
    pl.semaphore_wait(barrier, pairs - 1 + 2 + bits)

    def part_rows(index):
        return pl.ds(pl.multiple_of(index * part, part), part)

    scatter = []
    for step in range(1, pairs):
        other = lax.rem(depth + step, pairs)
        copy = pltpu.make_async_remote_copy(
            src_ref=sums_ref.at[part_rows(other)],
            dst_ref=zrecv.at[step - 1],
            send_sem=z_send.at[0, step - 1],
            recv_sem=z_recv.at[0, step - 1],
            device_id={"pairs": other},
            device_id_type=pl.DeviceIdType.MESH,
        )
        copy.start()
        scatter.append(copy)
    total = sums_ref[part_rows(depth), :]
    for step in range(1, pairs):
        scatter[step - 1].wait_recv()
        total = total + zrecv[step - 1]
    whole[part_rows(depth), :] = total
    gather = []
    for step in range(1, pairs):
        copy = pltpu.make_async_remote_copy(
            src_ref=whole.at[part_rows(depth)],
            dst_ref=whole.at[part_rows(depth)],
            send_sem=z_send.at[1, step - 1],
            recv_sem=z_recv.at[1, step - 1],
            device_id={"pairs": lax.rem(depth + step, pairs)},
            device_id_type=pl.DeviceIdType.MESH,
        )
        copy.start()
        gather.append(copy)
    for copy in gather:
        copy.wait_recv()

    latent = jnp.tanh(whole[:, :latents] + enc_bias_ref[...])
    latent_bf = latent.astype(jnp.bfloat16)
    seen = whole[:, latents:]
    seen_send[...] = jnp.concatenate([seen[:half], seen[half:]], axis=1)
    lat_send[...] = jnp.concatenate([latent_bf[:half], latent_bf[half:]], axis=1)
    sides = []
    for i, (source, target, other) in enumerate(
        [(seen_send, seen_recv, previous), (lat_send, lat_recv, following)]
    ):
        copy = pltpu.make_async_remote_copy(
            src_ref=source,
            dst_ref=target,
            send_sem=side_send.at[i],
            recv_sem=side_recv.at[i],
            device_id={"frames": other},
            device_id_type=pl.DeviceIdType.MESH,
        )
        copy.start()
        sides.append(copy)

    lag = lag_ref[...]
    scale = scale_ref[...]
    frame = lax.broadcasted_iota(jnp.int32, (rows, 1), 0)
    usable = me * rows + frame + lag < rows * frames
    used = jnp.where(usable, latent_bf.astype(jnp.float32), 0.0).astype(jnp.bfloat16)
    mix = lax.dot_general(used, used, (((0,), (0,)), ((), ())), preferred_element_type=jnp.float32)
    tilt = lax.dot_general(
        used, jnp.ones((rows, 128), jnp.bfloat16), (((0,), (0,)), ((), ())), preferred_element_type=jnp.float32
    )[:, :1]
    mix_parts = jnp.concatenate(split(mix, 3), axis=1)
    decoded = lean_ref[...]
    for piece in split(gram_ref[...], 3):
        decoded = decoded + jnp.dot(latent_bf, piece, preferred_element_type=jnp.float32)
    for copy in sides:
        copy.wait_recv()
    seen_all = jnp.concatenate([seen, seen_recv[:, :latents], seen_recv[:, latents:]], axis=0)
    latent_all = jnp.concatenate([lat_recv[:, :latents], lat_recv[:, latents:], latent_bf], axis=0)
    place = lax.broadcasted_iota(jnp.int32, (rows, 2 * rows), 1)
    pick_later = jnp.where(place == frame + lag, 1.0, 0.0).astype(jnp.bfloat16)
    pick_earlier = jnp.where(place == frame + rows - lag, 1.0, 0.0).astype(jnp.bfloat16)
    later = jnp.zeros((rows, latents), jnp.float32)
    for piece in split(seen_all, 3):
        later = later + jnp.dot(pick_later, piece, preferred_element_type=jnp.float32)
    earlier = jnp.dot(pick_earlier, latent_all, preferred_element_type=jnp.float32)
    earlier = jnp.where(me * rows + frame >= lag, earlier, 0.0)
    backward = jnp.where(usable, (decoded - later) * scale, 0.0)
    hidden = backward * (1.0 - latent * latent)
    left_ref[...] = jnp.transpose(jnp.concatenate([hidden, earlier], axis=1)).astype(jnp.bfloat16)
    load.wait()

    def order(color):
        turn = color % max(bits - 1, 1)
        later_bits = list(range(1, bits))
        return [0] + later_bits[turn:] + later_bits[:turn]

    def begin_of(sequence, count):
        begin = 0
        for k in range(count):
            begin = begin + bit_of(sequence[k]) * (frames >> (k + 1))
        return begin

    def halving(chunk, sequence, k):
        size = frames >> (k + 1)
        begin = begin_of(sequence, k) + (1 - bit_of(sequence[k])) * size
        return pltpu.make_async_remote_copy(
            src_ref=partial_sum.at[chunk, pl.ds(begin, size)],
            dst_ref=arrived.at[chunk, pl.ds(frames - 2 * size, size)],
            send_sem=half_send.at[chunk, k],
            recv_sem=half_recv.at[chunk, k],
            device_id={"frames": partner(sequence[k])},
            device_id_type=pl.DeviceIdType.MESH,
        )

    def doubling(chunk, sequence, k):
        size = frames >> (k + 1)
        columns = pl.ds(
            pl.multiple_of(chunk * width + begin_of(sequence, k + 1) * shard, shard), size * shard
        )
        return pltpu.make_async_remote_copy(
            src_ref=out_ref.at[:, columns],
            dst_ref=out_ref.at[:, columns],
            send_sem=full_send.at[chunk, k],
            recv_sem=full_recv.at[chunk, k],
            device_id={"frames": partner(sequence[k])},
            device_id_type=pl.DeviceIdType.MESH,
        )

    def each_chunk(body):
        def pair(index, carry):
            for color in range(2):
                body(index * 2 + color, order(color))
            return carry

        lax.fori_loop(0, chunks // 2, pair, 0)

    def multiply(chunk, sequence):
        columns = pl.ds(pl.multiple_of(chunk * width, width), width)
        product = jnp.dot(left_ref[...], contact_ref[:, columns], preferred_element_type=jnp.float32)
        dec = dec_ref[:, columns]
        own = jnp.dot(mix_parts, jnp.concatenate([dec, dec, dec], axis=0), preferred_element_type=jnp.float32)
        decode = scale * (own + tilt * bias_ref[:, columns] - product[latents:])
        for i in range(frames):
            here = slice(i * shard, (i + 1) * shard)
            partial_sum[chunk, i, :latents] = product[:latents, here]
            partial_sum[chunk, i, latents:] = decode[:, here]
        halving(chunk, sequence, 0).start()

    each_chunk(multiply)
    for k in range(bits):
        def reduce(chunk, sequence, k=k):
            halving(chunk, sequence, k).wait_recv()
            size = frames >> (k + 1)
            begin = begin_of(sequence, k + 1)
            added = partial_sum[chunk, pl.ds(begin, size)] + arrived[chunk, pl.ds(frames - 2 * size, size)]
            if k < bits - 1:
                partial_sum[chunk, pl.ds(begin, size)] = added
                halving(chunk, sequence, k + 1).start()
            else:
                columns = pl.ds(pl.multiple_of(chunk * width + begin * shard, shard), shard)
                out_ref[:, columns] = added[0]
                doubling(chunk, sequence, k).start()

        each_chunk(reduce)
    for k in reversed(range(bits)):
        def spread(chunk, sequence, k=k):
            doubling(chunk, sequence, k).wait_recv()
            if k > 0:
                doubling(chunk, sequence, k - 1).start()

        each_chunk(spread)

    def finish(chunk, sequence):
        for k in range(bits):
            halving(chunk, sequence, k).wait_send()
            doubling(chunk, sequence, k).wait_send()

    each_chunk(finish)
    for copy in scatter + gather + sides:
        copy.wait_send()


def tail(lag, scale, enc_bias, sums, gram, lean, dec_weight, dec_bias, contact):
    rows, pairs = contact.shape
    latents = dec_weight.shape[0]
    frames, depth = lax.axis_size("frames"), lax.axis_size("pairs")
    bits = frames.bit_length() - 1
    chunks = 2 * max(1, min(4, pairs // (2 * frames * 128)))
    shard = pairs // chunks // frames
    vmem = pl.BlockSpec(memory_space=pltpu.VMEM)
    dma = pltpu.SemaphoreType.DMA
    return pl.pallas_call(
        partial(tail_kernel, chunks),
        in_specs=[vmem] * 8 + [pl.BlockSpec(memory_space=pl.ANY)],
        out_specs=vmem,
        out_shape=jax.ShapeDtypeStruct((2 * latents, pairs), jnp.float32),
        scratch_shapes=[
            pltpu.VMEM((rows, pairs), jnp.bfloat16),
            pltpu.VMEM((depth - 1, rows // depth, 2 * latents), jnp.float32),
            pltpu.VMEM((rows, 2 * latents), jnp.float32),
            pltpu.VMEM((rows // 2, 2 * latents), jnp.float32),
            pltpu.VMEM((rows // 2, 2 * latents), jnp.float32),
            pltpu.VMEM((rows // 2, 2 * latents), jnp.bfloat16),
            pltpu.VMEM((rows // 2, 2 * latents), jnp.bfloat16),
            pltpu.VMEM((2 * latents, rows), jnp.bfloat16),
            pltpu.VMEM((chunks, frames, 2 * latents, shard), jnp.float32),
            pltpu.VMEM((chunks, frames - 1, 2 * latents, shard), jnp.float32),
            dma,
            dma((2, depth - 1)),
            dma((2, depth - 1)),
            dma((2,)),
            dma((2,)),
            dma((chunks, bits)),
            dma((chunks, bits)),
            dma((chunks, bits)),
            dma((chunks, bits)),
        ],
        compiler_params=pltpu.CompilerParams(
            vmem_limit_bytes=50 * 2**20, collective_id=0, has_side_effects=True
        ),
        name="tail",
    )(lag, scale, enc_bias, sums, gram, lean, dec_weight, dec_bias, contact)


def local(coords, pair_first, pair_second, enc_weight, enc_bias, dec_weight, dec_bias, lag_frames):
    rows = coords.shape[0]
    latents, pairs = enc_weight.shape
    total_frames = rows * lax.axis_size("frames")
    first = jnp.broadcast_to(pair_first[:, None], (pairs // 128, 128)).reshape(1, pairs)
    bias = dec_bias.reshape(1, pairs)
    gram = lax.dot_general(
        dec_weight, dec_weight, (((1,), (1,)), ((), ())), preferred_element_type=jnp.float32
    )
    lean = jnp.sum(dec_weight.astype(jnp.float32) * bias, axis=1)
    small = lax.psum(jnp.concatenate([gram, lean[None, :]]), "pairs")
    contact, sums = contacts(coords, first, pair_second.reshape(1, pairs), enc_weight, dec_weight)
    scale = 1.0 / jnp.sqrt(jnp.float32(total_frames) - lag_frames.astype(jnp.float32))
    both = tail(
        lag_frames.reshape(1, 1), scale.reshape(1, 1), enc_bias.reshape(1, latents), sums,
        small[:latents], small[latents:], dec_weight, bias, contact,
    )
    return both[:latents], both[latents:]


def solution(mesh):
    placed = (
        P("frames", None, None),
        P("pairs"),
        P("pairs"),
        P(None, "pairs"),
        P(),
        P(None, "pairs"),
        P("pairs"),
        P(),
    )
    return jax.shard_map(
        local,
        mesh=mesh,
        in_specs=placed,
        out_specs=(P(None, "pairs"), P(None, "pairs")),
        check_vma=False,
    )
```

time: 195 us -> 125 us (0.64)
  waiting for transfers between devices: 125 us -> 0 us
  Pallas kernels: 35.7 us -> 92.9 us
  blocking collectives: 0 us -> 21.2 us
  between operations: 14.9 us -> 1.58 us
  local copies, waits for them, and re-layouts: 14.3 us -> 5.41 us
  starting transfers between devices: 2.65 us -> 0 us
    psum x2 -> x0, waiting for transfers between devices: 122 us -> none  [the longest x1 84.4 us: local(): return tuple(lax.psum(tuple(both), 'frames'))]
    pallas_call x1, Pallas kernels: 5.13 us -> 62.8 us  [tail(): pl.pallas_call(partial(tail_kernel, chunks), in_specs=[vmem] * 8 + [pl.Bl...]
    psum x0 -> x1, blocking collectives: none -> 21.2 us  [local(): small = lax.psum(jnp.concatenate([gram, lean[None, :]]), 'pairs')]
    unnamed x22 -> x10, local copies, waits for them, and re-layouts: 12.1 us -> 0.03 us
    slice x5 -> x3, local copies, waits for them, and re-layouts: 0.14 us -> 4.64 us  [the longest x1 4.64 us: local(): return (both[:latents], both[latents:])]
    ppermute x2 -> x0, waiting for transfers between devices: 3.36 us -> none  [the longest x1 3.35 us: middle(): lax.ppermute(seen, 'frames', [(i, i - 1) for i in range(1, devices)])]
    ppermute x2 -> x0, starting transfers between devices: 2.57 us -> none  [the longest x1 1.29 us: middle(): lax.ppermute(latent_bf, 'frames', [(i, i + 1) for i in range(devices - 1)])]
  transfers between devices with their start and end apart: 4 -> 0, of which waited for: 3 -> 0; matrix products, arithmetic and copies ran while one was open for 0% -> 0% of each run, Pallas kernels for 0% -> 0%
where the time goes in v2:
time: 125 us
  Pallas kernels  92.9 us (74%)
  blocking collectives  21.2 us (17%)
  local copies, waits for them, and re-layouts  5.41 us (4%)
  matrix products  2.03 us (2%)
  between operations  1.58 us (1%)
  other arithmetic  1.54 us (1%)
    pallas_call x1, Pallas kernels, tail(): pl.pallas_call(partial(tail_kernel, chunks), in_specs=[vmem] * 8 + [pl.Bl...  62.8 us
    pallas_call x1, Pallas kernels, contacts(): pl.pallas_call(contact_kernel, grid=(pairs // width,), in_specs=[pl.Block...  30.1 us
    psum x1, blocking collectives, local(): small = lax.psum(jnp.concatenate([gram, lean[None, :]]), 'pairs')  21.2 us
    slice x1, local copies, waits for them, and re-layouts, local(): return (both[:latents], both[latents:])  4.64 us

profile of v2, /device:TPU:0, one launch (start us, length us, event | category | flops | bytes accessed | tf_op | source)
XLA Modules:
  0.0 124.7 jit_solution(114491988388230897)
XLA Ops:
  0.6 0.0 copy-start
  0.6 0.0 copy-start.3
  0.7 0.0 copy-start.4
  1.5 1.5 %multiply_reduce_fusion = f32[64]{0:T(128)S(1)} fusion(bf16[64,8192]{1,0:T(8,128)(2,1)} %dec_ref.3, f32[8192]{0:T(1024)} %param.14), kind=kLoop, calls=%fused_computation | loop fusion | flops 1572800 | bytes 1081600 | tf_op jit(solution)/shard_map/reduce_sum | solution.py:361
  3.0 0.7 broadcast_in_dim.4
  3.8 2.0 %fusion.1 = f32[64,64]{1,0:T(8,128)S(1)} fusion(bf16[64,8192]{1,0:T(8,128)(2,1)} %dec_ref.3), kind=kOutput, calls=%fused_computation.3 | convolution fusion | flops 67108864 | bytes 1064960 | tf_op jit(solution)/shard_map/dot_general | solution.py:358
  5.8 21.2 %psum.7 = f32[65,64]{1,0:T(8,128)S(1)} all-reduce(f32[65,64]{1,0:T(8,128)S(1)} %pad_maximum_fusion), channel_id=1, replica_groups=mesh['frames'=8,'pairs'=4] {'pairs'}, use_global_device_ids=true, to_apply=%region_1.0 | all-reduce | flops 4160 | bytes 33280 | tf_op jit(solution)/shard_map/psum | solution.py:362
  27.0 0.0 copy-done
  27.1 0.0 copy-done.3
  27.1 0.0 copy-done.4
  27.1 0.0 copy-start.1
  27.1 0.0 copy-start.2
  27.1 30.1 %contacts.1 = (bf16[512,8192]{1,0:T(8,128)(2,1)}, f32[512,128]{1,0:T(8,128)S(1)}) custom-call(f32[3,512,384]{2,1,0:T(8,128)} %bitcast.16, s32[1,8192]{1,0:T(1,128)S(1)} %bitcast.12, s32[1,8192]{1,0:T(1,128)S(1)} %bitcast.14, bf16[64,8192]{1,0:T(8,128)(2,1)S(1)} %copy-done.3, bf16[64,8192]{1,0:T(8,128)(2,1)S(1)} %copy-done), custom_call_target="tpu_custom_call" | custom-call | flops 19327352832 | bytes 16777216 | tf_op jit(solution)/shard_map/contacts/pallas_call | solution.py:74
  57.2 0.0 copy-done.1
  57.2 0.0 copy-done.2
  57.2 62.8 %tail.1 = f32[128,8192]{1,0:T(8,128)} custom-call(s32[1,1]{1,0:T(1,128)} %bitcast.10.lag_ref, f32[1,1]{1,0:T(1,128)} %bitcast.1.scale_ref, f32[1,64]{1,0:T(1,128)S(1)} %bitcast.13, f32[512,128]{1,0:T(8,128)S(1)} %get-tuple-element.4.sums_ref, f32[64,64]{1,0:T(8,128)S(1)} %slice.16.gram_ref, f32[1,64]{1,0:T(1,128)S(1)} %slice.17.lean_ref, ...), custom_call_target="tpu_custom_call" | custom-call | tf_op jit(solution)/shard_map/tail/pallas_call | solution.py:319
  120.0 4.6 %fusion = (f32[64,8192]{1,0:T(8,128)}, f32[64,8192]{1,0:T(8,128)}) fusion(f32[128,8192]{1,0:T(8,128)} %tail.1), kind=kLoop, calls=%fused_computation.2 | loop fusion | bytes 8388608 | tf_op jit(solution)/shard_map/slice | solution.py:369
  (3 shorter events, 0.0 us)
Async XLA Ops:
  0.6 26.4 %copy-start = (bf16[64,8192]{1,0:T(8,128)(2,1)S(1)}, bf16[64,8192]{1,0:T(8,128)(2,1)}, u32[]{:S(2)}) copy-start(bf16[64,8192]{1,0:T(8,128)(2,1)} %dec_ref.3) | copy-start | bytes 3145732
  0.6 26.4 %copy-start.3 = (bf16[64,8192]{1,0:T(8,128)(2,1)S(1)}, bf16[64,8192]{1,0:T(8,128)(2,1)}, u32[]{:S(2)}) copy-start(bf16[64,8192]{1,0:T(8,128)(2,1)} %enc_ref.1) | copy-start | bytes 3145732
  0.7 26.4 %copy-start.4 = (s32[8192]{0:T(1024)S(1)}, s32[8192]{0:T(1024)}, u32[]{:S(2)}) copy-start(s32[8192]{0:T(1024)} %param.10) | copy-start | bytes 98308
  27.1 30.1 %copy-start.1 = (f32[8192]{0:T(1024)S(1)}, f32[8192]{0:T(1024)}, u32[]{:S(2)}) copy-start(f32[8192]{0:T(1024)} %param.14) | copy-start | bytes 98308
  27.1 30.1 %copy-start.2 = (f32[64]{0:T(128)S(1)}, f32[64]{0:T(128)}, u32[]{:S(2)}) copy-start(f32[64]{0:T(128)} %param.12) | copy-start | bytes 772

commit v3 on v2

--- a/solution.py
+++ b/solution.py
@@ -25,7 +25,9 @@
 
 
 def contact_kernel(
-    coords_ref, first_ref, second_ref, enc_ref, dec_ref, contact_ref, sums_ref, table, weights
+    coords_ref, first_ref, second_ref, enc_ref, dec_ref, bias_ref, contact_ref, out_ref, table, weights,
+    sums_ref, gram_ref, lean_ref,
+
 ):
     step = pl.program_id(0)
     rows, residues = coords_ref.shape[1], coords_ref.shape[2]
@@ -36,11 +38,19 @@
             for i, part in enumerate(split(coords_ref[axis], pieces)):
                 table[axis * rows:(axis + 1) * rows, i * residues:(i + 1) * residues] = part
         sums_ref[...] = jnp.zeros_like(sums_ref)
+        gram_ref[...] = jnp.zeros_like(gram_ref)
+        lean_ref[...] = jnp.zeros_like(lean_ref)
 
     width = first_ref.shape[1]
     latents = enc_ref.shape[0]
     weights[:latents, :] = enc_ref[...]
     weights[latents:, :] = dec_ref[...]
+    gram_ref[...] += lax.dot_general(
+        dec_ref[...], dec_ref[...], (((1,), (1,)), ((), ())), preferred_element_type=jnp.float32
+    )
+    lean = dec_ref[...].astype(jnp.float32) * bias_ref[...]
+    for i in range(width // 128):
+        lean_ref[...] += lean[:, i * 128:(i + 1) * 128]
     total = jnp.zeros(sums_ref.shape, jnp.float32)
     for i in range(width // unit):
         here = slice(i * unit, (i + 1) * unit)
@@ -64,28 +74,43 @@
         )
     sums_ref[...] += total
 
-
-def contacts(coords, first, second, enc_weight, dec_weight):
+    @pl.when(step == pl.num_programs(0) - 1)
+    def finish():
+        parts = out_ref.shape[0]
+        part, few = rows // parts, latents // parts
+        lean = jnp.broadcast_to(jnp.sum(lean_ref[...], axis=1, keepdims=True), (latents, latents))
+        small = jnp.concatenate([gram_ref[...], lean], axis=1)
+        for i in range(parts):
+            out_ref[i, :part] = sums_ref[i * part:(i + 1) * part, :]
+            out_ref[i, part:] = small[i * few:(i + 1) * few]
+
+
+def contacts(coords, first, second, enc_weight, dec_weight, dec_bias):
     rows, _, residues = coords.shape
     latents, pairs = enc_weight.shape
     width = min(512, pairs)
+    parts = lax.axis_size("pairs")
+    sent = (parts, (rows + latents) // parts, 2 * latents)
     row = pl.BlockSpec((1, width), lambda i: (0, i))
     block = pl.BlockSpec((latents, width), lambda i: (0, i))
     return pl.pallas_call(
         contact_kernel,
         grid=(pairs // width,),
-        in_specs=[pl.BlockSpec((3, rows, residues), lambda i: (0, 0, 0)), row, row, block, block],
+        in_specs=[pl.BlockSpec((3, rows, residues), lambda i: (0, 0, 0)), row, row, block, block, row],
         out_specs=[
             pl.BlockSpec((rows, width), lambda i: (0, i)),
-            pl.BlockSpec((rows, 2 * latents), lambda i: (0, 0)),
+            pl.BlockSpec(sent, lambda i: (0, 0, 0)),
         ],
         out_shape=[
             jax.ShapeDtypeStruct((rows, pairs), jnp.bfloat16),
-            jax.ShapeDtypeStruct((rows, 2 * latents), jnp.float32),
+            jax.ShapeDtypeStruct(sent, jnp.float32),
         ],
         scratch_shapes=[
             pltpu.VMEM((3 * rows, pieces * residues), jnp.bfloat16),
             pltpu.VMEM((2 * latents, width), jnp.bfloat16),
+            pltpu.VMEM((rows, 2 * latents), jnp.float32),
+            pltpu.VMEM((latents, latents), jnp.float32),
+            pltpu.VMEM((latents, 128), jnp.float32),
         ],
         compiler_params=pltpu.CompilerParams(vmem_limit_bytes=50 * 2**20),
         cost_estimate=pl.CostEstimate(
@@ -94,18 +119,18 @@
             transcendentals=3 * rows * pairs,
         ),
         name="contacts",
-    )(jnp.transpose(coords, (1, 0, 2)), first, second, enc_weight, dec_weight)
+    )(jnp.transpose(coords, (1, 0, 2)), first, second, enc_weight, dec_weight, dec_bias)
 
 
 def tail_kernel(
-    chunks, lag_ref, scale_ref, enc_bias_ref, sums_ref, gram_ref, lean_ref, dec_ref, bias_ref, contact_any,
+    chunks, lag_ref, scale_ref, enc_bias_ref, sums_ref, dec_ref, bias_ref, contact_any,
     out_ref, contact_ref, zrecv, whole, seen_send, seen_recv, lat_send, lat_recv, left_ref, partial_sum, arrived,
     contact_sem, z_send, z_recv, side_send, side_recv, half_send, half_recv, full_send, full_recv,
 ):
     frames, pairs = lax.axis_size("frames"), lax.axis_size("pairs")
     me, depth = lax.axis_index("frames"), lax.axis_index("pairs")
     bits = frames.bit_length() - 1
-    rows, latents = sums_ref.shape[0], dec_ref.shape[0]
+    rows, latents = contact_any.shape[0], dec_ref.shape[0]
     part = rows // pairs
     width = dec_ref.shape[1] // chunks
     shard = width // frames
@@ -130,14 +155,11 @@
         pl.semaphore_signal(barrier, inc=1, device_id={"frames": other}, device_id_type=pl.DeviceIdType.MESH)
     pl.semaphore_wait(barrier, pairs - 1 + 2 + bits)
 
-    def part_rows(index):
-        return pl.ds(pl.multiple_of(index * part, part), part)
-
     scatter = []
     for step in range(1, pairs):
         other = lax.rem(depth + step, pairs)
         copy = pltpu.make_async_remote_copy(
-            src_ref=sums_ref.at[part_rows(other)],
+            src_ref=sums_ref.at[other],
             dst_ref=zrecv.at[step - 1],
             send_sem=z_send.at[0, step - 1],
             recv_sem=z_recv.at[0, step - 1],
@@ -146,16 +168,16 @@
         )
         copy.start()
         scatter.append(copy)
-    total = sums_ref[part_rows(depth), :]
+    total = sums_ref[depth]
     for step in range(1, pairs):
         scatter[step - 1].wait_recv()
         total = total + zrecv[step - 1]
-    whole[part_rows(depth), :] = total
+    whole[depth] = total
     gather = []
     for step in range(1, pairs):
         copy = pltpu.make_async_remote_copy(
-            src_ref=whole.at[part_rows(depth)],
-            dst_ref=whole.at[part_rows(depth)],
+            src_ref=whole.at[depth],
+            dst_ref=whole.at[depth],
             send_sem=z_send.at[1, step - 1],
             recv_sem=z_recv.at[1, step - 1],
             device_id={"pairs": lax.rem(depth + step, pairs)},
@@ -166,9 +188,13 @@
     for copy in gather:
         copy.wait_recv()
 
-    latent = jnp.tanh(whole[:, :latents] + enc_bias_ref[...])
+    sums = jnp.concatenate([whole[i, :part] for i in range(pairs)], axis=0)
+    small = jnp.concatenate([whole[i, part:] for i in range(pairs)], axis=0)
+    gram = small[:, :latents]
+    lean = jnp.transpose(small)[latents:latents + 1, :]
+    latent = jnp.tanh(sums[:, :latents] + enc_bias_ref[...])
     latent_bf = latent.astype(jnp.bfloat16)
-    seen = whole[:, latents:]
+    seen = sums[:, latents:]
     seen_send[...] = jnp.concatenate([seen[:half], seen[half:]], axis=1)
     lat_send[...] = jnp.concatenate([latent_bf[:half], latent_bf[half:]], axis=1)
     sides = []
@@ -196,8 +222,8 @@
         used, jnp.ones((rows, 128), jnp.bfloat16), (((0,), (0,)), ((), ())), preferred_element_type=jnp.float32
     )[:, :1]
     mix_parts = jnp.concatenate(split(mix, 3), axis=1)
-    decoded = lean_ref[...]
-    for piece in split(gram_ref[...], 3):
+    decoded = lean
+    for piece in split(gram, 3):
         decoded = decoded + jnp.dot(latent_bf, piece, preferred_element_type=jnp.float32)
     for copy in sides:
         copy.wait_recv()
@@ -307,7 +333,7 @@
         copy.wait_send()
 
 
-def tail(lag, scale, enc_bias, sums, gram, lean, dec_weight, dec_bias, contact):
+def tail(lag, scale, enc_bias, sums, dec_weight, dec_bias, contact):
     rows, pairs = contact.shape
     latents = dec_weight.shape[0]
     frames, depth = lax.axis_size("frames"), lax.axis_size("pairs")
@@ -318,13 +344,13 @@
     dma = pltpu.SemaphoreType.DMA
     return pl.pallas_call(
         partial(tail_kernel, chunks),
-        in_specs=[vmem] * 8 + [pl.BlockSpec(memory_space=pl.ANY)],
+        in_specs=[vmem] * 6 + [pl.BlockSpec(memory_space=pl.ANY)],
         out_specs=vmem,
         out_shape=jax.ShapeDtypeStruct((2 * latents, pairs), jnp.float32),
         scratch_shapes=[
             pltpu.VMEM((rows, pairs), jnp.bfloat16),
-            pltpu.VMEM((depth - 1, rows // depth, 2 * latents), jnp.float32),
-            pltpu.VMEM((rows, 2 * latents), jnp.float32),
+            pltpu.VMEM((depth - 1, *sums.shape[1:]), jnp.float32),
+            pltpu.VMEM(sums.shape, jnp.float32),
             pltpu.VMEM((rows // 2, 2 * latents), jnp.float32),
             pltpu.VMEM((rows // 2, 2 * latents), jnp.float32),
             pltpu.VMEM((rows // 2, 2 * latents), jnp.bfloat16),
@@ -346,7 +372,7 @@
             vmem_limit_bytes=50 * 2**20, collective_id=0, has_side_effects=True
         ),
         name="tail",
-    )(lag, scale, enc_bias, sums, gram, lean, dec_weight, dec_bias, contact)
+    )(lag, scale, enc_bias, sums, dec_weight, dec_bias, contact)
 
 
 def local(coords, pair_first, pair_second, enc_weight, enc_bias, dec_weight, dec_bias, lag_frames):
@@ -355,16 +381,11 @@
     total_frames = rows * lax.axis_size("frames")
     first = jnp.broadcast_to(pair_first[:, None], (pairs // 128, 128)).reshape(1, pairs)
     bias = dec_bias.reshape(1, pairs)
-    gram = lax.dot_general(
-        dec_weight, dec_weight, (((1,), (1,)), ((), ())), preferred_element_type=jnp.float32
-    )
-    lean = jnp.sum(dec_weight.astype(jnp.float32) * bias, axis=1)
-    small = lax.psum(jnp.concatenate([gram, lean[None, :]]), "pairs")
-    contact, sums = contacts(coords, first, pair_second.reshape(1, pairs), enc_weight, dec_weight)
+    contact, sums = contacts(coords, first, pair_second.reshape(1, pairs), enc_weight, dec_weight, bias)
     scale = 1.0 / jnp.sqrt(jnp.float32(total_frames) - lag_frames.astype(jnp.float32))
     both = tail(
         lag_frames.reshape(1, 1), scale.reshape(1, 1), enc_bias.reshape(1, latents), sums,
-        small[:latents], small[latents:], dec_weight, bias, contact,
+        dec_weight, bias, contact,
     )
     return both[:latents], both[latents:]
 

time: 125 us -> 109 us (0.87)
  blocking collectives: 21.2 us -> 0 us
  Pallas kernels: 92.9 us -> 97.6 us
  local copies, waits for them, and re-layouts: 5.41 us -> 9.34 us
  matrix products: 2.03 us -> 0 us
  other arithmetic: 1.54 us -> 0 us
    psum x1 -> x0, blocking collectives: 21.2 us -> none  [local(): small = lax.psum(jnp.concatenate([gram, lean[None, :]]), 'pairs')]
    unnamed x10 -> x12, local copies, waits for them, and re-layouts: 0.03 us -> 3.98 us
    pallas_call x1, Pallas kernels: 62.8 us -> 66.7 us  [tail(): pl.pallas_call(partial(tail_kernel, chunks), in_specs=[vmem] * 6 + [pl.Bl...]
    dot_general x1 -> x0, matrix products: 2.03 us -> none  [local(): lax.dot_general(dec_weight, dec_weight, (((1,), (1,)), ((), ())), preferr...]
    reduce_sum x1 -> x0, other arithmetic: 1.53 us -> none  [local(): lean = jnp.sum(dec_weight.astype(jnp.float32) * bias, axis=1)]
where the time goes in v3:
time: 109 us; the launch traced here: 108 us
  Pallas kernels  97.6 us (90%)
  local copies, waits for them, and re-layouts  9.34 us (9%)
  between operations  1.33 us (1%)
    pallas_call x1, Pallas kernels, tail(): pl.pallas_call(partial(tail_kernel, chunks), in_specs=[vmem] * 6 + [pl.Bl...  66.7 us
    pallas_call x1, Pallas kernels, contacts(): pl.pallas_call(contact_kernel, grid=(pairs // width,), in_specs=[pl.Block...  30.9 us
    slice x1, local copies, waits for them, and re-layouts, local(): return (both[:latents], both[latents:])  4.64 us
    unnamed x12, local copies, waits for them, and re-layouts  3.98 us

profile of v3, /device:TPU:0, one launch (start us, length us, event | category | flops | bytes accessed | tf_op | source)
XLA Modules:
  0.0 108.2 jit_solution(1285576194950575957)
XLA Ops:
  1.3 0.7 broadcast_in_dim.2
  2.0 0.0 copy-start
  2.0 1.2 %copy-done = bf16[64,8192]{1,0:T(8,128)(2,1)S(1)} copy-done((bf16[64,8192]{1,0:T(8,128)(2,1)S(1)}, bf16[64,8192]{1,0:T(8,128)(2,1)}, u32[]{:S(2)}) %copy-start) | copy-done | bytes 1048600
  3.3 0.0 copy-start.2
  3.3 0.8 copy-done.2
  4.0 0.0 copy-start.4
  4.0 1.2 %copy-done.4 = bf16[64,8192]{1,0:T(8,128)(2,1)S(1)} copy-done((bf16[64,8192]{1,0:T(8,128)(2,1)S(1)}, bf16[64,8192]{1,0:T(8,128)(2,1)}, u32[]{:S(2)}) %copy-start.4) | copy-done | bytes 1048600
  5.3 0.0 copy-start.5
  5.3 0.8 copy-done.5
  6.0 0.0 copy-start.1
  6.0 0.0 copy-start.3
  6.0 30.9 %contacts.1 = (bf16[512,8192]{1,0:T(8,128)(2,1)}, f32[4,144,128]{2,1,0:T(8,128)S(1)}) custom-call(f32[3,512,384]{2,1,0:T(8,128)} %bitcast.13, s32[1,8192]{1,0:T(1,128)S(1)} %bitcast.10, s32[1,8192]{1,0:T(1,128)S(1)} %bitcast.12, bf16[64,8192]{1,0:T(8,128)(2,1)S(1)} %copy-done.4, bf16[64,8192]{1,0:T(8,128)(2,1)S(1)} %copy-done, f32[1,8192]{1,0:T(1,128)S(1)} %bitcast.8), custom_call_target="tpu_custom_call" | custom-call | flops 19327352832 | bytes 16777216 | tf_op jit(solution)/shard_map/contacts/pallas_call | solution.py:96
  36.9 0.0 copy-done.1
  36.9 0.0 copy-done.3
  36.9 66.7 %tail.1 = f32[128,8192]{1,0:T(8,128)} custom-call(s32[1,1]{1,0:T(1,128)} %bitcast.7.lag_ref, f32[1,1]{1,0:T(1,128)} %bitcast.1.scale_ref, f32[1,64]{1,0:T(1,128)S(1)} %bitcast.11, f32[4,144,128]{2,1,0:T(8,128)S(1)} %get-tuple-element.4.sums_ref, bf16[64,8192]{1,0:T(8,128)(2,1)S(1)} %copy-done.1, f32[1,8192]{1,0:T(1,128)S(1)} %bitcast.9, ...), custom_call_target="tpu_custom_call" | custom-call | tf_op jit(solution)/shard_map/tail/pallas_call | solution.py:345
  103.6 4.6 %fusion = (f32[64,8192]{1,0:T(8,128)}, f32[64,8192]{1,0:T(8,128)}) fusion(f32[128,8192]{1,0:T(8,128)} %tail.1), kind=kLoop, calls=%fused_computation | loop fusion | bytes 8388608 | tf_op jit(solution)/shard_map/slice | solution.py:390
Async XLA Ops:
  2.0 1.2 %copy-start = (bf16[64,8192]{1,0:T(8,128)(2,1)S(1)}, bf16[64,8192]{1,0:T(8,128)(2,1)}, u32[]{:S(2)}) copy-start(bf16[64,8192]{1,0:T(8,128)(2,1)} %dec_ref.3) | copy-start | bytes 3145732
  3.3 0.8 copy-start.2
  4.0 1.2 %copy-start.4 = (bf16[64,8192]{1,0:T(8,128)(2,1)S(1)}, bf16[64,8192]{1,0:T(8,128)(2,1)}, u32[]{:S(2)}) copy-start(bf16[64,8192]{1,0:T(8,128)(2,1)} %enc_ref.1) | copy-start | bytes 3145732
  5.3 0.8 copy-start.5
  6.0 30.9 %copy-start.1 = (bf16[64,8192]{1,0:T(8,128)(2,1)S(1)}, bf16[64,8192]{1,0:T(8,128)(2,1)}, u32[]{:S(2)}) copy-start(bf16[64,8192]{1,0:T(8,128)(2,1)} %dec_ref.3) | copy-start | bytes 3145732
  6.0 30.9 %copy-start.3 = (f32[64]{0:T(128)S(1)}, f32[64]{0:T(128)}, u32[]{:S(2)}) copy-start(f32[64]{0:T(128)} %param.12) | copy-start | bytes 772

commit v4 on v3

--- a/solution.py
+++ b/solution.py
@@ -122,9 +122,34 @@
     )(jnp.transpose(coords, (1, 0, 2)), first, second, enc_weight, dec_weight, dec_bias)
 
 
+def encode(value, latents):
+    size, width = value.shape[0], value.shape[-1]
+    peaks = [
+        jnp.maximum(jnp.max(jnp.max(jnp.abs(rows), axis=0), axis=0, keepdims=True), 1e-30)
+        for rows in (value[:, :latents], value[:, latents:])
+    ]
+    both = lambda low, high, rows: jnp.concatenate(
+        [jnp.broadcast_to(low, (rows, width)), jnp.broadcast_to(high, (rows, width))], axis=0
+    )
+    factor = both(32767.0 / peaks[0], 32767.0 / peaks[1], latents)
+    codes = jnp.round(value * factor[None]).astype(jnp.int32).astype(jnp.int16)
+    first_rows = lax.broadcasted_iota(jnp.int32, (8, width), 0) < 4
+    steps = jnp.where(first_rows, peaks[0] * (1.0 / 32767.0), peaks[1] * (1.0 / 32767.0))
+    return codes, steps
+
+
+def decode(codes, steps, latents):
+    width = steps.shape[-1]
+    factor = jnp.concatenate(
+        [jnp.broadcast_to(steps[:1], (latents, width)), jnp.broadcast_to(steps[4:5], (latents, width))], axis=0
+    )
+    return codes.astype(jnp.int32).astype(jnp.float32) * factor
+
+
 def tail_kernel(
     chunks, lag_ref, scale_ref, enc_bias_ref, sums_ref, dec_ref, bias_ref, contact_any,
-    out_ref, contact_ref, zrecv, whole, seen_send, seen_recv, lat_send, lat_recv, left_ref, partial_sum, arrived,
+    out_ref, step_ref, contact_ref, zrecv, whole, seen_send, seen_recv, lat_send, lat_recv, left_ref,
+    partial_sum, arrived, code_send, step_send, code_recv, step_recv,
     contact_sem, z_send, z_recv, side_send, side_recv, half_send, half_recv, full_send, full_recv,
 ):
     frames, pairs = lax.axis_size("frames"), lax.axis_size("pairs")
@@ -253,31 +278,47 @@
             begin = begin + bit_of(sequence[k]) * (frames >> (k + 1))
         return begin
 
+    def remote(source, target, sender, receiver, bit):
+        return pltpu.make_async_remote_copy(
+            src_ref=source,
+            dst_ref=target,
+            send_sem=sender,
+            recv_sem=receiver,
+            device_id={"frames": partner(bit)},
+            device_id_type=pl.DeviceIdType.MESH,
+        )
+
     def halving(chunk, sequence, k):
         size = frames >> (k + 1)
-        begin = begin_of(sequence, k) + (1 - bit_of(sequence[k])) * size
-        return pltpu.make_async_remote_copy(
-            src_ref=partial_sum.at[chunk, pl.ds(begin, size)],
-            dst_ref=arrived.at[chunk, pl.ds(frames - 2 * size, size)],
-            send_sem=half_send.at[chunk, k],
-            recv_sem=half_recv.at[chunk, k],
-            device_id={"frames": partner(sequence[k])},
-            device_id_type=pl.DeviceIdType.MESH,
-        )
+        if k == 0:
+            begin = (1 - bit_of(sequence[0])) * size
+            return [
+                remote(
+                    partial_sum.at[chunk, pl.ds(begin, size)], arrived.at[chunk],
+                    half_send.at[0, chunk, k], half_recv.at[0, chunk, k], sequence[k],
+                )
+            ]
+        here = pl.ds(frames // 2 - 2 * size, size)
+        return [
+            remote(
+                code_send.at[chunk, here], code_recv.at[chunk, here],
+                half_send.at[0, chunk, k], half_recv.at[0, chunk, k], sequence[k],
+            ),
+            remote(
+                step_send.at[chunk, k - 1], step_recv.at[chunk, k - 1],
+                half_send.at[1, chunk, k], half_recv.at[1, chunk, k], sequence[k],
+            ),
+        ]
 
     def doubling(chunk, sequence, k):
-        size = frames >> (k + 1)
-        columns = pl.ds(
-            pl.multiple_of(chunk * width + begin_of(sequence, k + 1) * shard, shard), size * shard
-        )
-        return pltpu.make_async_remote_copy(
-            src_ref=out_ref.at[:, columns],
-            dst_ref=out_ref.at[:, columns],
-            send_sem=full_send.at[chunk, k],
-            recv_sem=full_recv.at[chunk, k],
-            device_id={"frames": partner(sequence[k])},
-            device_id_type=pl.DeviceIdType.MESH,
-        )
+        here = pl.ds(begin_of(sequence, k + 1), frames >> (k + 1))
+        return [
+            remote(
+                ref.at[chunk, here], ref.at[chunk, here],
+                full_send.at[i, chunk, k], full_recv.at[i, chunk, k], sequence[k],
+            )
+            for i, ref in enumerate((out_ref, step_ref))
+        ]
 
     def each_chunk(body):
         def pair(index, carry):
@@ -297,36 +338,54 @@
             here = slice(i * shard, (i + 1) * shard)
             partial_sum[chunk, i, :latents] = product[:latents, here]
             partial_sum[chunk, i, latents:] = decode[:, here]
-        halving(chunk, sequence, 0).start()
+        for copy in halving(chunk, sequence, 0):
+            copy.start()
 
     each_chunk(multiply)
     for k in range(bits):
         def reduce(chunk, sequence, k=k):
-            halving(chunk, sequence, k).wait_recv()
+            for copy in halving(chunk, sequence, k):
+                copy.wait_recv()
             size = frames >> (k + 1)
             begin = begin_of(sequence, k + 1)
-            added = partial_sum[chunk, pl.ds(begin, size)] + arrived[chunk, pl.ds(frames - 2 * size, size)]
+            if k == 0:
+                came = arrived[chunk]
+            else:
+                codes = code_recv[chunk, pl.ds(frames // 2 - 2 * size, size)]
+                came = decode(codes, step_recv[chunk, k - 1], latents)
+            added = partial_sum[chunk, pl.ds(begin, size)] + came
             if k < bits - 1:
+                half_size = size // 2
+                turn = bit_of(sequence[k + 1])
                 partial_sum[chunk, pl.ds(begin, size)] = added
-                halving(chunk, sequence, k + 1).start()
+                leaving = partial_sum[chunk, pl.ds(begin + (1 - turn) * half_size, half_size)]
+                codes, steps = encode(leaving, latents)
+                code_send[chunk, pl.ds(frames // 2 - 2 * half_size, half_size)] = codes
+                step_send[chunk, k] = steps
+                for copy in halving(chunk, sequence, k + 1):
+                    copy.start()
             else:
-                columns = pl.ds(pl.multiple_of(chunk * width + begin * shard, shard), shard)
-                out_ref[:, columns] = added[0]
-                doubling(chunk, sequence, k).start()
+                codes, steps = encode(added, latents)
+                out_ref[chunk, pl.ds(begin, 1)] = codes
+                step_ref[chunk, begin] = steps
+                for copy in doubling(chunk, sequence, k):
+                    copy.start()
 
         each_chunk(reduce)
     for k in reversed(range(bits)):
         def spread(chunk, sequence, k=k):
-            doubling(chunk, sequence, k).wait_recv()
+            for copy in doubling(chunk, sequence, k):
+                copy.wait_recv()
             if k > 0:
-                doubling(chunk, sequence, k - 1).start()
+                for copy in doubling(chunk, sequence, k - 1):
+                    copy.start()
 
         each_chunk(spread)
 
     def finish(chunk, sequence):
         for k in range(bits):
-            halving(chunk, sequence, k).wait_send()
-            doubling(chunk, sequence, k).wait_send()
+            for copy in halving(chunk, sequence, k) + doubling(chunk, sequence, k):
+                copy.wait_send()
 
     each_chunk(finish)
     for copy in scatter + gather + sides:
@@ -345,8 +404,11 @@
     return pl.pallas_call(
         partial(tail_kernel, chunks),
         in_specs=[vmem] * 6 + [pl.BlockSpec(memory_space=pl.ANY)],
-        out_specs=vmem,
-        out_shape=jax.ShapeDtypeStruct((2 * latents, pairs), jnp.float32),
+        out_specs=[vmem, vmem],
+        out_shape=[
+            jax.ShapeDtypeStruct((chunks, frames, 2 * latents, shard), jnp.int16),
+            jax.ShapeDtypeStruct((chunks, frames, 8, shard), jnp.float32),
+        ],
         scratch_shapes=[
             pltpu.VMEM((rows, pairs), jnp.bfloat16),
             pltpu.VMEM((depth - 1, *sums.shape[1:]), jnp.float32),
@@ -357,22 +419,52 @@
             pltpu.VMEM((rows // 2, 2 * latents), jnp.bfloat16),
             pltpu.VMEM((2 * latents, rows), jnp.bfloat16),
             pltpu.VMEM((chunks, frames, 2 * latents, shard), jnp.float32),
-            pltpu.VMEM((chunks, frames - 1, 2 * latents, shard), jnp.float32),
+            pltpu.VMEM((chunks, frames // 2, 2 * latents, shard), jnp.float32),
+            pltpu.VMEM((chunks, max(1, frames // 2 - 1), 2 * latents, shard), jnp.int16),
+            pltpu.VMEM((chunks, max(1, bits - 1), 8, shard), jnp.float32),
+            pltpu.VMEM((chunks, max(1, frames // 2 - 1), 2 * latents, shard), jnp.int16),
+            pltpu.VMEM((chunks, max(1, bits - 1), 8, shard), jnp.float32),
             dma,
             dma((2, depth - 1)),
             dma((2, depth - 1)),
             dma((2,)),
             dma((2,)),
-            dma((chunks, bits)),
-            dma((chunks, bits)),
-            dma((chunks, bits)),
-            dma((chunks, bits)),
+            dma((2, chunks, bits)),
+            dma((2, chunks, bits)),
+            dma((2, chunks, bits)),
+            dma((2, chunks, bits)),
         ],
         compiler_params=pltpu.CompilerParams(
             vmem_limit_bytes=50 * 2**20, collective_id=0, has_side_effects=True
         ),
         name="tail",
     )(lag, scale, enc_bias, sums, dec_weight, dec_bias, contact)
+
+
+def decode_kernel(code_ref, step_ref, enc_out, dec_out):
+    frames, shard = code_ref.shape[1], code_ref.shape[3]
+    latents = enc_out.shape[0]
+    for i in range(frames):
+        value = decode(code_ref[0, i], step_ref[0, i], latents)
+        enc_out[:, i * shard:(i + 1) * shard] = value[:latents]
+        dec_out[:, i * shard:(i + 1) * shard] = value[latents:]
+
+
+def decoded_outputs(codes, steps):
+    chunks, frames, rows, shard = codes.shape
+    latents, width = rows // 2, frames * shard
+    out = pl.BlockSpec((latents, width), lambda i: (0, i))
+    return pl.pallas_call(
+        decode_kernel,
+        grid=(chunks,),
+        in_specs=[
+            pl.BlockSpec((1, frames, rows, shard), lambda i: (i, 0, 0, 0)),
+            pl.BlockSpec((1, frames, 8, shard), lambda i: (i, 0, 0, 0)),
+        ],
+        out_specs=[out, out],
+        out_shape=[jax.ShapeDtypeStruct((latents, chunks * width), jnp.float32)] * 2,
+        name="decode",
+    )(codes, steps)
 
 
 def local(coords, pair_first, pair_second, enc_weight, enc_bias, dec_weight, dec_bias, lag_frames):
@@ -383,11 +475,11 @@
     bias = dec_bias.reshape(1, pairs)
     contact, sums = contacts(coords, first, pair_second.reshape(1, pairs), enc_weight, dec_weight, bias)
     scale = 1.0 / jnp.sqrt(jnp.float32(total_frames) - lag_frames.astype(jnp.float32))
-    both = tail(
+    codes, steps = tail(
         lag_frames.reshape(1, 1), scale.reshape(1, 1), enc_bias.reshape(1, latents), sums,
         dec_weight, bias, contact,
     )
-    return both[:latents], both[latents:]
+    return tuple(decoded_outputs(codes, steps))
 
 
 def solution(mesh):

time: 109 us -> 96 us (0.88)
  Pallas kernels: 97.6 us -> 87.5 us
  local copies, waits for them, and re-layouts: 9.34 us -> 6.73 us
    pallas_call x1, Pallas kernels: 66.7 us -> 50.5 us  [tail(): pl.pallas_call(partial(tail_kernel, chunks), in_specs=[vmem] * 6 + [pl.Bl...]
    pallas_call x0 -> x1, Pallas kernels: none -> 6.08 us  [decoded_outputs(): pl.pallas_call(decode_kernel, grid=(chunks,), in_specs=[pl.BlockSpec((1,...]
    slice x1 -> x0, local copies, waits for them, and re-layouts: 4.64 us -> none  [local(): return (both[:latents], both[latents:])]
    unnamed x12 -> x18, local copies, waits for them, and re-layouts: 3.98 us -> 6 us
where the time goes in v4:
time: 96 us; the launch traced here: 95.5 us
  Pallas kernels  87.5 us (91%)
  local copies, waits for them, and re-layouts  6.73 us (7%)
  between operations  1.35 us (1%)
    pallas_call x1, Pallas kernels, tail(): pl.pallas_call(partial(tail_kernel, chunks), in_specs=[vmem] * 6 + [pl.Bl...  50.5 us
    pallas_call x1, Pallas kernels, contacts(): pl.pallas_call(contact_kernel, grid=(pairs // width,), in_specs=[pl.Block...  30.9 us
    pallas_call x1, Pallas kernels, decoded_outputs(): pl.pallas_call(decode_kernel, grid=(chunks,), in_specs=[pl.BlockSpec((1,...  6.08 us
    unnamed x18, local copies, waits for them, and re-layouts  6 us

profile of v4, /device:TPU:0, one launch (start us, length us, event | category | flops | bytes accessed | tf_op | source)
XLA Modules:
  0.0 95.5 jit_solution(5714658385441894586)
XLA Ops:
  1.3 0.7 broadcast_in_dim.2
  2.0 0.0 copy-start.1
  2.0 1.2 %copy-done.1 = bf16[64,8192]{1,0:T(8,128)(2,1)S(1)} copy-done((bf16[64,8192]{1,0:T(8,128)(2,1)S(1)}, bf16[64,8192]{1,0:T(8,128)(2,1)}, u32[]{:S(2)}) %copy-start.1) | copy-done | bytes 1048600
  3.3 0.0 copy-start.4
  3.3 0.8 copy-done.4
  4.0 0.0 copy-start.7
  4.0 1.2 %copy-done.7 = bf16[64,8192]{1,0:T(8,128)(2,1)S(1)} copy-done((bf16[64,8192]{1,0:T(8,128)(2,1)S(1)}, bf16[64,8192]{1,0:T(8,128)(2,1)}, u32[]{:S(2)}) %copy-start.7) | copy-done | bytes 1048600
  5.3 0.0 copy-start.8
  5.3 0.8 copy-done.8
  6.0 0.0 copy-start.2
  6.0 0.0 copy-start.5
  6.0 0.0 copy-start.6
  6.0 30.9 %contacts.1 = (bf16[512,8192]{1,0:T(8,128)(2,1)}, f32[4,144,128]{2,1,0:T(8,128)S(1)}) custom-call(f32[3,512,384]{2,1,0:T(8,128)} %bitcast.13, s32[1,8192]{1,0:T(1,128)S(1)} %bitcast.8, s32[1,8192]{1,0:T(1,128)S(1)} %bitcast.12, bf16[64,8192]{1,0:T(8,128)(2,1)S(1)} %copy-done.7, bf16[64,8192]{1,0:T(8,128)(2,1)S(1)} %copy-done.1, f32[1,8192]{1,0:T(1,128)S(1)} %bitcast.9), custom_call_target="tpu_custom_call" | custom-call | flops 19327352832 | bytes 16777216 | tf_op jit(solution)/shard_map/contacts/pallas_call | solution.py:96
  36.9 0.0 copy-done.2
  36.9 0.0 copy-done.5
  36.9 0.0 copy-done.6
  36.9 50.5 %tail.1 = (s16[8,8,128,128]{3,2,1,0:T(8,128)(2,1)S(1)}, f32[8,8,8,128]{3,2,1,0:T(8,128)S(1)}) custom-call(s32[1,1]{1,0:T(1,128)} %bitcast.7.lag_ref, f32[1,1]{1,0:T(1,128)} %bitcast.1.scale_ref, f32[1,64]{1,0:T(1,128)S(1)} %bitcast.11, f32[4,144,128]{2,1,0:T(8,128)S(1)} %get-tuple-element.6.sums_ref, bf16[64,8192]{1,0:T(8,128)(2,1)S(1)} %copy-done.2, ...), custom_call_target="tpu_custom_call" | custom-call | tf_op jit(solution)/shard_map/tail/pallas_call | solution.py:404
  87.4 0.0 copy-start
  87.4 1.3 %copy-done = s16[8,8,128,128]{3,2,1,0:T(8,128)(2,1)} copy-done((s16[8,8,128,128]{3,2,1,0:T(8,128)(2,1)}, s16[8,8,128,128]{3,2,1,0:T(8,128)(2,1)S(1)}, u32[]{:S(2)}) %copy-start) | copy-done | bytes 2097176
  88.8 0.0 copy-start.3
  88.8 0.7 copy-done.3
  89.5 6.1 %decode.1 = (f32[64,8192]{1,0:T(8,128)}, f32[64,8192]{1,0:T(8,128)}) custom-call(s16[8,8,128,128]{3,2,1,0:T(8,128)(2,1)} %copy-done, f32[8,8,8,128]{3,2,1,0:T(8,128)} %copy-done.3), custom_call_target="tpu_custom_call" | custom-call | tf_op jit(solution)/shard_map/decode/pallas_call | solution.py:457
Async XLA Ops:
  2.0 1.2 %copy-start.1 = (bf16[64,8192]{1,0:T(8,128)(2,1)S(1)}, bf16[64,8192]{1,0:T(8,128)(2,1)}, u32[]{:S(2)}) copy-start(bf16[64,8192]{1,0:T(8,128)(2,1)} %dec_ref.3) | copy-start | bytes 3145732
  3.3 0.8 copy-start.4
  4.0 1.2 %copy-start.7 = (bf16[64,8192]{1,0:T(8,128)(2,1)S(1)}, bf16[64,8192]{1,0:T(8,128)(2,1)}, u32[]{:S(2)}) copy-start(bf16[64,8192]{1,0:T(8,128)(2,1)} %enc_ref.1) | copy-start | bytes 3145732
  5.3 0.8 copy-start.8
  6.0 30.9 %copy-start.2 = (bf16[64,8192]{1,0:T(8,128)(2,1)S(1)}, bf16[64,8192]{1,0:T(8,128)(2,1)}, u32[]{:S(2)}) copy-start(bf16[64,8192]{1,0:T(8,128)(2,1)} %dec_ref.3) | copy-start | bytes 3145732
  6.0 30.9 %copy-start.5 = (f32[8192]{0:T(1024)S(1)}, f32[8192]{0:T(1024)}, u32[]{:S(2)}) copy-start(f32[8192]{0:T(1024)} %param.14) | copy-start | bytes 98308
  6.0 30.9 %copy-start.6 = (f32[64]{0:T(128)S(1)}, f32[64]{0:T(128)}, u32[]{:S(2)}) copy-start(f32[64]{0:T(128)} %param.12) | copy-start | bytes 772
  87.4 1.3 %copy-start = (s16[8,8,128,128]{3,2,1,0:T(8,128)(2,1)}, s16[8,8,128,128]{3,2,1,0:T(8,128)(2,1)S(1)}, u32[]{:S(2)}) copy-start(s16[8,8,128,128]{3,2,1,0:T(8,128)(2,1)S(1)} %get-tuple-element.8.code_ref) | copy-start | bytes 6291460
  88.8 0.7 copy-start.3

commit v5 on v4

--- a/solution.py
+++ b/solution.py
@@ -41,7 +41,7 @@
         gram_ref[...] = jnp.zeros_like(gram_ref)
         lean_ref[...] = jnp.zeros_like(lean_ref)
 
-    width = first_ref.shape[1]
+    width = second_ref.shape[1]
     latents = enc_ref.shape[0]
     weights[:latents, :] = enc_ref[...]
     weights[latents:, :] = dec_ref[...]
@@ -55,9 +55,14 @@
     for i in range(width // unit):
         here = slice(i * unit, (i + 1) * unit)
         ids = lax.broadcasted_iota(jnp.int32, (residues, unit), 0)
-        choice = (
-            jnp.where(ids == second_ref[:, here], 1.0, 0.0) - jnp.where(ids == first_ref[:, here], 1.0, 0.0)
-        ).astype(jnp.bfloat16)
+        near = jnp.concatenate(
+            [
+                jnp.where(ids[:, :128] == first_ref[(step * width + i * unit) // 128 + j], 1.0, 0.0)
+                for j in range(unit // 128)
+            ],
+            axis=1,
+        )
+        choice = (jnp.where(ids == second_ref[:, here], 1.0, 0.0) - near).astype(jnp.bfloat16)
         choice = jnp.concatenate([choice] * pieces, axis=0)
         square = jnp.zeros((rows, unit), jnp.float32)
         for axis in range(3):
@@ -67,7 +72,7 @@
             square = square + offset * offset
         distance = square * lax.rsqrt(jnp.maximum(square, 1e-30))
         power = jnp.exp2(distance * (log2_e / softness) - cutoff_dist * log2_e / softness)
-        contact = (1.0 / (1.0 + power)).astype(jnp.bfloat16)
+        contact = pltpu.reciprocal(1.0 + power, approx=True).astype(jnp.bfloat16)
         contact_ref[:, here] = contact
         total = total + lax.dot_general(
             contact, weights[:, here], (((1,), (1,)), ((), ())), preferred_element_type=jnp.float32
@@ -88,7 +93,7 @@
 def contacts(coords, first, second, enc_weight, dec_weight, dec_bias):
     rows, _, residues = coords.shape
     latents, pairs = enc_weight.shape
-    width = min(512, pairs)
+    width = min(2048, pairs)
     parts = lax.axis_size("pairs")
     sent = (parts, (rows + latents) // parts, 2 * latents)
     row = pl.BlockSpec((1, width), lambda i: (0, i))
@@ -96,7 +101,7 @@
     return pl.pallas_call(
         contact_kernel,
         grid=(pairs // width,),
-        in_specs=[pl.BlockSpec((3, rows, residues), lambda i: (0, 0, 0)), row, row, block, block, row],
+        in_specs=[pl.BlockSpec((3, rows, residues), lambda i: (0, 0, 0)), pl.BlockSpec(memory_space=pltpu.SMEM), row, block, block, row],
         out_specs=[
             pl.BlockSpec((rows, width), lambda i: (0, i)),
             pl.BlockSpec(sent, lambda i: (0, 0, 0)),
@@ -112,7 +117,7 @@
             pltpu.VMEM((latents, latents), jnp.float32),
             pltpu.VMEM((latents, 128), jnp.float32),
         ],
-        compiler_params=pltpu.CompilerParams(vmem_limit_bytes=50 * 2**20),
+        compiler_params=pltpu.CompilerParams(vmem_limit_bytes=60 * 2**20),
         cost_estimate=pl.CostEstimate(
             flops=2 * 3 * rows * pieces * residues * pairs,
             bytes_accessed=4 * rows * pairs,
@@ -435,34 +440,55 @@
             dma((2, chunks, bits)),
         ],
         compiler_params=pltpu.CompilerParams(
-            vmem_limit_bytes=50 * 2**20, collective_id=0, has_side_effects=True
+            vmem_limit_bytes=60 * 2**20, collective_id=0, has_side_effects=True
         ),
         name="tail",
     )(lag, scale, enc_bias, sums, dec_weight, dec_bias, contact)
 
 
-def decode_kernel(code_ref, step_ref, enc_out, dec_out):
-    frames, shard = code_ref.shape[1], code_ref.shape[3]
-    latents = enc_out.shape[0]
-    for i in range(frames):
-        value = decode(code_ref[0, i], step_ref[0, i], latents)
-        enc_out[:, i * shard:(i + 1) * shard] = value[:latents]
-        dec_out[:, i * shard:(i + 1) * shard] = value[latents:]
+def decode_kernel(code_ref, step_ref, enc_out, dec_out, values, sems):
+    chunks, frames, rows, shard = code_ref.shape
+    latents, width = rows // 2, frames * shard
+
+    def leave(chunk):
+        here = pl.ds(pl.multiple_of(chunk * width, width), width)
+        return [
+            pltpu.make_async_copy(values.at[chunk, i], out.at[:, here], sems.at[i, chunk])
+            for i, out in enumerate((enc_out, dec_out))
+        ]
+
+    def one(chunk, carry):
+        for i in range(frames):
+            value = decode(code_ref[chunk, i], step_ref[chunk, i], latents)
+            values[chunk, 0, :, i * shard:(i + 1) * shard] = value[:latents]
+            values[chunk, 1, :, i * shard:(i + 1) * shard] = value[latents:]
+        for copy in leave(chunk):
+            copy.start()
+        return carry
+
+    lax.fori_loop(0, chunks, one, 0)
+
+    def end(chunk, carry):
+        for copy in leave(chunk):
+            copy.wait()
+        return carry
+
+    lax.fori_loop(0, chunks, end, 0)
 
 
 def decoded_outputs(codes, steps):
     chunks, frames, rows, shard = codes.shape
     latents, width = rows // 2, frames * shard
-    out = pl.BlockSpec((latents, width), lambda i: (0, i))
     return pl.pallas_call(
         decode_kernel,
-        grid=(chunks,),
-        in_specs=[
-            pl.BlockSpec((1, frames, rows, shard), lambda i: (i, 0, 0, 0)),
-            pl.BlockSpec((1, frames, 8, shard), lambda i: (i, 0, 0, 0)),
+        in_specs=[pl.BlockSpec(memory_space=pltpu.VMEM)] * 2,
+        out_specs=[pl.BlockSpec(memory_space=pl.ANY)] * 2,
+        out_shape=[jax.ShapeDtypeStruct((latents, chunks * width), jnp.float32)] * 2,
+        scratch_shapes=[
+            pltpu.VMEM((chunks, 2, latents, width), jnp.float32),
+            pltpu.SemaphoreType.DMA((2, chunks)),
         ],
-        out_specs=[out, out],
-        out_shape=[jax.ShapeDtypeStruct((latents, chunks * width), jnp.float32)] * 2,
+        compiler_params=pltpu.CompilerParams(vmem_limit_bytes=24 * 2**20),
         name="decode",
     )(codes, steps)
 
@@ -471,9 +497,8 @@
     rows = coords.shape[0]
     latents, pairs = enc_weight.shape
     total_frames = rows * lax.axis_size("frames")
-    first = jnp.broadcast_to(pair_first[:, None], (pairs // 128, 128)).reshape(1, pairs)
     bias = dec_bias.reshape(1, pairs)
-    contact, sums = contacts(coords, first, pair_second.reshape(1, pairs), enc_weight, dec_weight, bias)
+    contact, sums = contacts(coords, pair_first, pair_second.reshape(1, pairs), enc_weight, dec_weight, bias)
     scale = 1.0 / jnp.sqrt(jnp.float32(total_frames) - lag_frames.astype(jnp.float32))
     codes, steps = tail(
         lag_frames.reshape(1, 1), scale.reshape(1, 1), enc_bias.reshape(1, latents), sums,

time: 96 us -> 96.5 us (level)
  Pallas kernels: 87.5 us -> 92.4 us
  local copies, waits for them, and re-layouts: 6.73 us -> 2.53 us
    pallas_call x1, Pallas kernels: 30.9 us -> 36.8 us  [contacts(): pl.pallas_call(contact_kernel, grid=(pairs // width,), in_specs=[pl.Block...]
    pallas_call x1, Pallas kernels: 6.08 us -> 2.2 us  [decoded_outputs(): pl.pallas_call(decode_kernel, in_specs=[pl.BlockSpec(memory_space=pltpu.V...]
    unnamed x18 -> x4, local copies, waits for them, and re-layouts: 6 us -> 2.53 us
    pallas_call x1, Pallas kernels: 50.5 us -> 53.3 us  [tail(): pl.pallas_call(partial(tail_kernel, chunks), in_specs=[vmem] * 6 + [pl.Bl...]
where the time goes in v5:
time: 96.5 us; the launch traced here: 96.2 us
  Pallas kernels  92.4 us (96%)
  local copies, waits for them, and re-layouts  2.53 us (3%)
  between operations  1.34 us (1%)
    pallas_call x1, Pallas kernels, tail(): pl.pallas_call(partial(tail_kernel, chunks), in_specs=[vmem] * 6 + [pl.Bl...  53.3 us
    pallas_call x1, Pallas kernels, contacts(): pl.pallas_call(contact_kernel, grid=(pairs // width,), in_specs=[pl.Block...  36.8 us
    unnamed x4, local copies, waits for them, and re-layouts  2.53 us
    pallas_call x1, Pallas kernels, decoded_outputs(): pl.pallas_call(decode_kernel, in_specs=[pl.BlockSpec(memory_space=pltpu.V...  2.2 us

profile of v5, /device:TPU:0, one launch (start us, length us, event | category | flops | bytes accessed | tf_op | source)
XLA Modules:
  0.0 96.2 jit_solution(9132547142187444895)
XLA Ops:
  1.3 36.8 %contacts.1 = (bf16[512,8192]{1,0:T(8,128)(2,1)}, f32[4,144,128]{2,1,0:T(8,128)}) custom-call(f32[3,512,384]{2,1,0:T(8,128)} %bitcast.10, s32[64]{0:T(128)} %first_ref.1, s32[1,8192]{1,0:T(1,128)} %bitcast.11, bf16[64,8192]{1,0:T(8,128)(2,1)} %enc_ref.1, bf16[64,8192]{1,0:T(8,128)(2,1)} %dec_ref.3, f32[1,8192]{1,0:T(1,128)} %bitcast.7), custom_call_target="tpu_custom_call" | custom-call | flops 19327352832 | bytes 16777216 | tf_op jit(solution)/shard_map/contacts/pallas_call | solution.py:101
  38.2 53.3 %tail.1 = (s16[8,8,128,128]{3,2,1,0:T(8,128)(2,1)}, f32[8,8,8,128]{3,2,1,0:T(8,128)}) custom-call(s32[1,1]{1,0:T(1,128)} %bitcast.6.lag_ref, f32[1,1]{1,0:T(1,128)} %bitcast.1.scale_ref, f32[1,64]{1,0:T(1,128)} %bitcast.9, f32[4,144,128]{2,1,0:T(8,128)} %get-tuple-element.6.sums_ref, bf16[64,8192]{1,0:T(8,128)(2,1)} %dec_ref.3, f32[1,8192]{1,0:T(1,128)} %bitcast.8, ...), custom_call_target="tpu_custom_call" | custom-call | tf_op jit(solution)/shard_map/tail/pallas_call | solution.py:409
  91.5 0.0 copy-start
  91.5 1.6 %copy-done = s16[8,8,128,128]{3,2,1,0:T(8,128)(2,1)S(1)} copy-done((s16[8,8,128,128]{3,2,1,0:T(8,128)(2,1)S(1)}, s16[8,8,128,128]{3,2,1,0:T(8,128)(2,1)}, u32[]{:S(2)}) %copy-start) | copy-done | bytes 2097176
  93.1 0.0 copy-start.1
  93.1 0.9 copy-done.1
  94.0 2.2 %decode.1 = (f32[64,8192]{1,0:T(8,128)}, f32[64,8192]{1,0:T(8,128)}) custom-call(s16[8,8,128,128]{3,2,1,0:T(8,128)(2,1)S(1)} %copy-done, f32[8,8,8,128]{3,2,1,0:T(8,128)S(1)} %copy-done.1), custom_call_target="tpu_custom_call" | custom-call | tf_op jit(solution)/shard_map/decode/pallas_call | solution.py:482
Async XLA Ops:
  91.5 1.6 %copy-start = (s16[8,8,128,128]{3,2,1,0:T(8,128)(2,1)S(1)}, s16[8,8,128,128]{3,2,1,0:T(8,128)(2,1)}, u32[]{:S(2)}) copy-start(s16[8,8,128,128]{3,2,1,0:T(8,128)(2,1)} %get-tuple-element.8.code_ref) | copy-start | bytes 6291460
  93.1 0.9 copy-start.1

commit v6 on v5

--- a/solution.py
+++ b/solution.py
@@ -72,7 +72,7 @@
             square = square + offset * offset
         distance = square * lax.rsqrt(jnp.maximum(square, 1e-30))
         power = jnp.exp2(distance * (log2_e / softness) - cutoff_dist * log2_e / softness)
-        contact = pltpu.reciprocal(1.0 + power, approx=True).astype(jnp.bfloat16)
+        contact = (1.0 / (1.0 + power)).astype(jnp.bfloat16)
         contact_ref[:, here] = contact
         total = total + lax.dot_general(
             contact, weights[:, here], (((1,), (1,)), ((), ())), preferred_element_type=jnp.float32
@@ -93,7 +93,7 @@
 def contacts(coords, first, second, enc_weight, dec_weight, dec_bias):
     rows, _, residues = coords.shape
     latents, pairs = enc_weight.shape
-    width = min(2048, pairs)
+    width = min(512, pairs)
     parts = lax.axis_size("pairs")
     sent = (parts, (rows + latents) // parts, 2 * latents)
     row = pl.BlockSpec((1, width), lambda i: (0, i))
@@ -152,10 +152,10 @@
 
 
 def tail_kernel(
-    chunks, lag_ref, scale_ref, enc_bias_ref, sums_ref, dec_ref, bias_ref, contact_any,
-    out_ref, step_ref, contact_ref, zrecv, whole, seen_send, seen_recv, lat_send, lat_recv, left_ref,
+    chunks, lag_ref, scale_ref, enc_bias_ref, sums_ref, bias_ref, dec_any, contact_any,
+    out_ref, step_ref, contact_ref, dec_ref, zrecv, whole, seen_send, seen_recv, lat_send, lat_recv, left_ref,
     partial_sum, arrived, code_send, step_send, code_recv, step_recv,
-    contact_sem, z_send, z_recv, side_send, side_recv, half_send, half_recv, full_send, full_recv,
+    load_sem, z_send, z_recv, side_send, side_recv, half_send, half_recv, full_send, full_recv,
 ):
     frames, pairs = lax.axis_size("frames"), lax.axis_size("pairs")
     me, depth = lax.axis_index("frames"), lax.axis_index("pairs")
@@ -174,8 +174,12 @@
 
     following, previous = lax.rem(me + 1, frames), lax.rem(me + frames - 1, frames)
 
-    load = pltpu.make_async_copy(contact_any, contact_ref, contact_sem)
-    load.start()
+    loads = [
+        pltpu.make_async_copy(dec_any, dec_ref, load_sem.at[0]),
+        pltpu.make_async_copy(contact_any, contact_ref, load_sem.at[1]),
+    ]
+    for copy in loads:
+        copy.start()
     barrier = pltpu.get_barrier_semaphore()
     for step in range(1, pairs):
         pl.semaphore_signal(
@@ -270,7 +274,8 @@
     backward = jnp.where(usable, (decoded - later) * scale, 0.0)
     hidden = backward * (1.0 - latent * latent)
     left_ref[...] = jnp.transpose(jnp.concatenate([hidden, earlier], axis=1)).astype(jnp.bfloat16)
-    load.wait()
+    for copy in loads:
+        copy.wait()
 
     def order(color):
         turn = color % max(bits - 1, 1)
@@ -408,7 +413,7 @@
     dma = pltpu.SemaphoreType.DMA
     return pl.pallas_call(
         partial(tail_kernel, chunks),
-        in_specs=[vmem] * 6 + [pl.BlockSpec(memory_space=pl.ANY)],
+        in_specs=[vmem] * 5 + [pl.BlockSpec(memory_space=pl.ANY)] * 2,
         out_specs=[vmem, vmem],
         out_shape=[
             jax.ShapeDtypeStruct((chunks, frames, 2 * latents, shard), jnp.int16),
@@ -416,6 +421,7 @@
         ],
         scratch_shapes=[
             pltpu.VMEM((rows, pairs), jnp.bfloat16),
+            pltpu.VMEM(dec_weight.shape, jnp.bfloat16),
             pltpu.VMEM((depth - 1, *sums.shape[1:]), jnp.float32),
             pltpu.VMEM(sums.shape, jnp.float32),
             pltpu.VMEM((rows // 2, 2 * latents), jnp.float32),
@@ -429,7 +435,7 @@
             pltpu.VMEM((chunks, max(1, bits - 1), 8, shard), jnp.float32),
             pltpu.VMEM((chunks, max(1, frames // 2 - 1), 2 * latents, shard), jnp.int16),
             pltpu.VMEM((chunks, max(1, bits - 1), 8, shard), jnp.float32),
-            dma,
+            dma((2,)),
             dma((2, depth - 1)),
             dma((2, depth - 1)),
             dma((2,)),
@@ -443,11 +449,11 @@
             vmem_limit_bytes=60 * 2**20, collective_id=0, has_side_effects=True
         ),
         name="tail",
-    )(lag, scale, enc_bias, sums, dec_weight, dec_bias, contact)
-
-
-def decode_kernel(code_ref, step_ref, enc_out, dec_out, values, sems):
-    chunks, frames, rows, shard = code_ref.shape
+    )(lag, scale, enc_bias, sums, dec_bias, dec_weight, contact)
+
+
+def decode_kernel(code_any, step_any, enc_out, dec_out, code_ref, step_ref, values, come_sems, sems):
+    chunks, frames, rows, shard = code_any.shape
     latents, width = rows // 2, frames * shard
 
     def leave(chunk):
@@ -457,7 +463,22 @@
             for i, out in enumerate((enc_out, dec_out))
         ]
 
+    def enter(chunk):
+        return [
+            pltpu.make_async_copy(code_any.at[chunk], code_ref.at[chunk], come_sems.at[0, chunk]),
+            pltpu.make_async_copy(step_any.at[chunk], step_ref.at[chunk], come_sems.at[1, chunk]),
+        ]
+
+    def begin(chunk, carry):
+        for copy in enter(chunk):
+            copy.start()
+        return carry
+
+    lax.fori_loop(0, chunks, begin, 0)
+
     def one(chunk, carry):
+        for copy in enter(chunk):
+            copy.wait()
         for i in range(frames):
             value = decode(code_ref[chunk, i], step_ref[chunk, i], latents)
             values[chunk, 0, :, i * shard:(i + 1) * shard] = value[:latents]
@@ -481,14 +502,17 @@
     latents, width = rows // 2, frames * shard
     return pl.pallas_call(
         decode_kernel,
-        in_specs=[pl.BlockSpec(memory_space=pltpu.VMEM)] * 2,
+        in_specs=[pl.BlockSpec(memory_space=pl.ANY)] * 2,
         out_specs=[pl.BlockSpec(memory_space=pl.ANY)] * 2,
         out_shape=[jax.ShapeDtypeStruct((latents, chunks * width), jnp.float32)] * 2,
         scratch_shapes=[
+            pltpu.VMEM(codes.shape, codes.dtype),
+            pltpu.VMEM(steps.shape, steps.dtype),
             pltpu.VMEM((chunks, 2, latents, width), jnp.float32),
             pltpu.SemaphoreType.DMA((2, chunks)),
+            pltpu.SemaphoreType.DMA((2, chunks)),
         ],
-        compiler_params=pltpu.CompilerParams(vmem_limit_bytes=24 * 2**20),
+        compiler_params=pltpu.CompilerParams(vmem_limit_bytes=60 * 2**20),
         name="decode",
     )(codes, steps)
 

time: 96.5 us -> 89 us (0.922)
  Pallas kernels: 92.4 us -> 87.5 us
  local copies, waits for them, and re-layouts: 2.53 us -> 0 us
    pallas_call x1, Pallas kernels: 36.8 us -> 31.2 us  [contacts(): pl.pallas_call(contact_kernel, grid=(pairs // width,), in_specs=[pl.Block...]
    unnamed x4 -> x0, local copies, waits for them, and re-layouts: 2.53 us -> none
where the time goes in v6:
time: 89 us; the launch traced here: 88.8 us
  Pallas kernels  87.5 us (98%)
  between operations  1.33 us (1%)
    pallas_call x1, Pallas kernels, tail(): pl.pallas_call(partial(tail_kernel, chunks), in_specs=[vmem] * 5 + [pl.Bl...  52.9 us
    pallas_call x1, Pallas kernels, contacts(): pl.pallas_call(contact_kernel, grid=(pairs // width,), in_specs=[pl.Block...  31.2 us
    pallas_call x1, Pallas kernels, decoded_outputs(): pl.pallas_call(decode_kernel, in_specs=[pl.BlockSpec(memory_space=pl.ANY)...  3.29 us

profile of v6, /device:TPU:0, one launch (start us, length us, event | category | flops | bytes accessed | tf_op | source)
XLA Modules:
  0.0 88.8 jit_solution(10391797310627538940)
XLA Ops:
  1.3 31.2 %contacts.1 = (bf16[512,8192]{1,0:T(8,128)(2,1)}, f32[4,144,128]{2,1,0:T(8,128)}) custom-call(f32[3,512,384]{2,1,0:T(8,128)} %bitcast.10, s32[64]{0:T(128)} %first_ref.1, s32[1,8192]{1,0:T(1,128)} %bitcast.11, bf16[64,8192]{1,0:T(8,128)(2,1)} %enc_ref.1, bf16[64,8192]{1,0:T(8,128)(2,1)} %dec_any.1, f32[1,8192]{1,0:T(1,128)} %bitcast.7), custom_call_target="tpu_custom_call" | custom-call | flops 19327352832 | bytes 16777216 | tf_op jit(solution)/shard_map/contacts/pallas_call | solution.py:101
  32.6 52.9 %tail.1 = (s16[8,8,128,128]{3,2,1,0:T(8,128)(2,1)}, f32[8,8,8,128]{3,2,1,0:T(8,128)}) custom-call(s32[1,1]{1,0:T(1,128)} %bitcast.6.lag_ref, f32[1,1]{1,0:T(1,128)} %bitcast.1.scale_ref, f32[1,64]{1,0:T(1,128)} %bitcast.9, f32[4,144,128]{2,1,0:T(8,128)} %get-tuple-element.6.sums_ref, f32[1,8192]{1,0:T(1,128)} %bitcast.8, bf16[64,8192]{1,0:T(8,128)(2,1)} %dec_any.1, ...), custom_call_target="tpu_custom_call" | custom-call | tf_op jit(solution)/shard_map/tail/pallas_call | solution.py:414
  85.5 3.3 %decode.1 = (f32[64,8192]{1,0:T(8,128)}, f32[64,8192]{1,0:T(8,128)}) custom-call(s16[8,8,128,128]{3,2,1,0:T(8,128)(2,1)} %get-tuple-element.8.code_any, f32[8,8,8,128]{3,2,1,0:T(8,128)} %get-tuple-element.9.step_any), custom_call_target="tpu_custom_call" | custom-call | tf_op jit(solution)/shard_map/decode/pallas_call | solution.py:503
